TPU v7x, 32 devices: a whole 2x2x4 slice. The times are simulated.
32 devices in a mesh: fsdp: 4 (over z), seq: 8 (over y, x, core).
Axes of the slice: x: 2, y: 2, z: 4, core: 2. Of those that a mesh axis runs over, the one named last changes fastest.
Arguments:
- query_teacher: bfloat16 [4, 1024, 4096], P('fsdp', 'seq'), may hold values from -180 to 180
- key_teacher: bfloat16 [4, 1024, 4096], P('fsdp', 'seq'), may hold values from -180 to 180
- value_teacher: bfloat16 [4, 1024, 4096], P('fsdp', 'seq'), may hold values from -36 to 36
- query_student: bfloat16 [4, 1024, 4096], P('fsdp', 'seq'), may hold values from -180 to 180
- key_student: bfloat16 [4, 1024, 4096], P('fsdp', 'seq'), may hold values from -180 to 180
- value_student: bfloat16 [4, 1024, 4096], P('fsdp', 'seq'), may hold values from -36 to 36
- timesteps: int32 [4], P('fsdp'), may hold values from 0 to 49
- student_gain: float32 [2, 4096], P(None, 'fsdp'), may hold values from 0.1 to 1.9
- ema_gain: float32 [2, 4096], P(None, 'fsdp'), may hold values from 0.1 to 1.9
Outputs:
- student_out: bfloat16 [4, 1024, 4096], P('fsdp', 'seq')
- clip_loss: float32 [4], P('fsdp')
- gain_grad: float32 [2, 4096], P(None, 'fsdp')
- new_student: float32 [2, 4096], P(None, 'fsdp')
- new_ema: float32 [2, 4096], replicated
All inputs are finite; a program needn't handle non-finite values.
Results may differ from a plain program's by a relative error of at most 0.019.
The roundings to bfloat16 on the way count: a program that leaves them out, or rounds other values in their place, can miss the bound.
Values may be sent and summed in bfloat16 or wider, within the bound.
No kernel may reach another device: no remote copies, remote signals or barrier semaphores. Data moves between devices by JAX's collectives and lax.ppermute only.
A program may use at most 128 MiB of HBM per device.

v0:
```python
import functools
import math

import jax
import jax.numpy as jnp
from jax import lax
from jax.experimental import pallas as pl
from jax.experimental.pallas import tpu as pltpu
from jax.sharding import PartitionSpec as P

HEAD_DIM = 128
TSTEPS = 50

norm_eps = 1e-06
step_size = 0.01
ema_decay = 0.95

VMEM_BYTES = 48 * 1024 * 1024
QUERY_BLOCK = 256

f32 = jnp.float32
bf16 = jnp.bfloat16


def params(limit=VMEM_BYTES):
    return pltpu.CompilerParams(vmem_limit_bytes=limit)


def cost(flops, nbytes, exps=0):
    return pl.CostEstimate(flops=flops, bytes_accessed=nbytes, transcendentals=exps)


def swap(x, axis, step):
    size = lax.axis_size(axis)
    return lax.ppermute(x, axis, [(i, i ^ step) for i in range(size)])


def nt(a, b):
    return lax.dot_general(a, b, (((1,), (1,)), ((), ())), preferred_element_type=f32)


def nn(a, b):
    return lax.dot_general(a, b, (((1,), (0,)), ((), ())), preferred_element_type=f32)


def prep_kernel(groups, width, plans, *refs):
    ins, outs = refs[:3], refs[3:]
    me = lax.axis_index("seq")
    inverse = []
    for x_ref in ins[:2]:
        wide = x_ref[...].astype(f32)
        inverse.append(lax.rsqrt(jnp.mean(wide * wide, axis=-1, keepdims=True) + norm_eps))

    at = 0
    for first, columns, by_step in plans:
        for slot in range(groups):
            if by_step:
                col = pl.multiple_of((me ^ slot) * width + first, HEAD_DIM)
            else:
                col = slot * width + first
            for a in range(3):
                part = ins[a][:, pl.ds(col, columns)]
                if a < 2:
                    part = (part.astype(f32) * inverse[a]).astype(bf16)
                if by_step:
                    outs[at + slot][a] = part
                else:
                    outs[at][slot, a] = part
        at += groups if by_step else 1


def prep(q, k, v, groups, width, plans):
    tokens, inner = q.shape
    rows = min(32, tokens)
    shapes, specs = [], []
    for _, columns, by_step in plans:
        if by_step:
            for _ in range(groups):
                shapes.append(jax.ShapeDtypeStruct((3, tokens, columns), bf16))
                specs.append(pl.BlockSpec((3, rows, columns), lambda i: (0, i, 0)))
        else:
            shapes.append(jax.ShapeDtypeStruct((groups, 3, tokens, columns), bf16))
            specs.append(pl.BlockSpec((groups, 3, rows, columns), lambda i: (0, 0, i, 0)))
    return pl.pallas_call(
        functools.partial(prep_kernel, groups, width, plans),
        grid=(tokens // rows,),
        in_specs=[pl.BlockSpec((rows, inner), lambda i: (i, 0))] * 3,
        out_specs=specs,
        out_shape=shapes,
        compiler_params=params(),
        cost_estimate=cost(20 * tokens * inner, 12 * tokens * inner),
        name="prep",
    )(q, k, v)


def part_at(refs, me, slot, a):
    if len(refs) > 1:
        return refs[slot][a]
    return refs[0][me ^ slot, a]


def load(refs, me, groups, tokens, gains, q_scr, k_scr, v_scr):
    for slot in range(groups):
        rows = pl.ds(slot * tokens, tokens)
        q_scr[rows, :] = (part_at(refs, me, slot, 0).astype(f32) * gains[0]).astype(bf16)
        k_scr[rows, :] = (part_at(refs, me, slot, 1).astype(f32) * gains[1]).astype(bf16)
        v_scr[rows, :] = part_at(refs, me, slot, 2)


def head_gains(gain_ref, me, width, column):
    col = pl.multiple_of(me * width + column, HEAD_DIM)
    return gain_ref[:, pl.ds(col, HEAD_DIM)]


def probabilities(q, k):
    factor = HEAD_DIM ** (-0.5) * math.log2(math.e)
    scores = nt(q, k)
    top = jnp.max(scores, axis=-1, keepdims=True)
    raised = jnp.exp2((scores - top) * factor)
    total = jnp.sum(raised, axis=-1, keepdims=True)
    return raised * (1.0 / total), top * factor + jnp.log2(total)


def student_kernel(groups, tokens, width, n_in, *refs):
    ins = refs[:n_in]
    gain_ref, out_ref, lse_ref, q_scr, k_scr, v_scr = refs[n_in:]
    me = lax.axis_index("seq")
    gains = head_gains(gain_ref, me, width, pl.program_id(0) * HEAD_DIM)
    load(ins, me, groups, tokens, (gains[0:1], gains[1:2]), q_scr, k_scr, v_scr)
    length = groups * tokens
    block = min(QUERY_BLOCK, length)
    for start in range(0, length, block):
        rows = pl.ds(start, block)
        probs, lse = probabilities(q_scr[rows, :], k_scr[...])
        out = nn(probs.astype(bf16), v_scr[...]).astype(bf16)
        lse_ref[0, rows, :] = jnp.broadcast_to(lse, (block, HEAD_DIM))
        for j in range(block // tokens):
            out_ref[me ^ (start // tokens + j)] = out[j * tokens : (j + 1) * tokens]


def chunk_specs(arrays, groups, tokens, first):
    if len(arrays) > 1:
        return [pl.BlockSpec((3, tokens, HEAD_DIM), lambda h: (0, 0, first + h))] * groups
    return [pl.BlockSpec((groups, 3, tokens, HEAD_DIM), lambda h: (0, 0, 0, first + h))]


def student(arrays, gains, groups, tokens, width):
    heads = width // HEAD_DIM
    length = groups * tokens
    work = length * length * heads
    return pl.pallas_call(
        functools.partial(student_kernel, groups, tokens, width, len(arrays)),
        grid=(heads,),
        in_specs=chunk_specs(arrays, groups, tokens, 0) + [pl.BlockSpec(gains.shape, lambda h: (0, 0))],
        out_specs=[
            pl.BlockSpec((groups, tokens, HEAD_DIM), lambda h: (0, 0, h)),
            pl.BlockSpec((1, length, HEAD_DIM), lambda h: (h, 0, 0)),
        ],
        out_shape=[
            jax.ShapeDtypeStruct((groups, tokens, width), bf16),
            jax.ShapeDtypeStruct((heads, length, HEAD_DIM), f32),
        ],
        scratch_shapes=[pltpu.VMEM((length, HEAD_DIM), bf16)] * 3,
        compiler_params=params(),
        cost_estimate=cost(8 * HEAD_DIM * work, 8 * length * width, work),
        name="student",
    )(*arrays, gains)


def teacher_kernel(groups, tokens, width, first, n_teacher, n_student, has_before, *refs):
    step_ref, *refs = refs
    teacher_refs, refs = refs[:n_teacher], refs[n_teacher:]
    student_refs, refs = refs[:n_student], refs[n_student:]
    gain_ref, out_ref, lse_ref, *refs = refs
    if has_before:
        before_ref, *refs = refs
    grad_ref, qt, kt, vt, qs, ks, vs = refs
    length = groups * tokens
    block = min(QUERY_BLOCK, length)
    scale = HEAD_DIM ** (-0.5)
    factor = scale * math.log2(math.e)
    head = pl.program_id(0)
    me = lax.axis_index("seq")
    column = (first + head) * HEAD_DIM
    gains = head_gains(gain_ref, me, width, column)
    load(teacher_refs, me, groups, tokens, (gains[2:3], gains[3:4]), qt, kt, vt)
    load(student_refs, me, groups, tokens, (gains[0:1], gains[1:2]), qs, ks, vs)
    step = jnp.full((1, HEAD_DIM), step_ref[0], jnp.int32).astype(f32)
    weight = 1.0 / (0.05 + (step + 1.0) / TSTEPS)
    share = weight / (length * (groups * width // HEAD_DIM))

    if has_before:

        @pl.when(head == 0)
        def _():
            grad_ref[...] = before_ref[...]

    else:

        @pl.when(head == 0)
        def _():
            grad_ref[...] = jnp.zeros_like(grad_ref)

    squares = jnp.zeros((1, HEAD_DIM), f32)
    term_q = jnp.zeros((1, HEAD_DIM), f32)
    key_grad = None
    for start in range(0, length, block):
        rows = pl.ds(start, block)
        slots = range(start // tokens, start // tokens + block // tokens)
        probs, _ = probabilities(qt[rows, :], kt[...])
        target = nn(probs.astype(bf16), vt[...]).astype(bf16)
        out = jnp.concatenate([out_ref[me ^ slot] for slot in slots], axis=0)
        diff = out.astype(f32) - target.astype(f32)
        squares = squares + jnp.sum(diff * diff, axis=0, keepdims=True)
        error = (2.0 * share * diff).astype(bf16)
        lse = lse_ref[0, rows, :][:, :1]
        probs = jnp.exp2(nt(qs[rows, :], ks[...]) * factor - lse)
        dprob = nt(error, vs[...])
        inner = jnp.sum(probs * dprob, axis=-1, keepdims=True)
        dscore = (probs * (dprob - inner)).astype(bf16)
        dquery = (nn(dscore, ks[...]) * scale).astype(bf16)
        unit = jnp.concatenate([part_at(student_refs, me, slot, 0) for slot in slots], axis=0)
        term_q = term_q + jnp.sum(dquery.astype(f32) * unit.astype(f32), axis=0, keepdims=True)
        part = nn(jnp.transpose(qs[rows, :]), dscore)
        key_grad = part if key_grad is None else key_grad + part
    dkey = (jnp.transpose(key_grad) * scale).astype(bf16)
    unit = jnp.concatenate([part_at(student_refs, me, slot, 1) for slot in range(groups)], axis=0)
    term_k = jnp.sum(dkey.astype(f32) * unit.astype(f32), axis=0, keepdims=True)
    cols = pl.ds(pl.multiple_of(column, HEAD_DIM), HEAD_DIM)
    grad_ref[0:1, cols] = term_q
    grad_ref[1:2, cols] = term_k
    grad_ref[2:3, cols] = share * squares


def teacher(timesteps, arrays, student_arrays, gains, out, lse, before, first, heads, groups, tokens, width):
    length = groups * tokens
    work = length * length * heads
    extra = [] if before is None else [before]
    return pl.pallas_call(
        functools.partial(
            teacher_kernel, groups, tokens, width, first, len(arrays), len(student_arrays), before is not None
        ),
        grid=(heads,),
        in_specs=[pl.BlockSpec(memory_space=pltpu.SMEM)]
        + chunk_specs(arrays, groups, tokens, 0)
        + chunk_specs(student_arrays, groups, tokens, first)
        + [
            pl.BlockSpec(gains.shape, lambda h: (0, 0)),
            pl.BlockSpec((groups, tokens, HEAD_DIM), lambda h: (0, 0, first + h)),
            pl.BlockSpec((1, length, HEAD_DIM), lambda h: (first + h, 0, 0)),
        ]
        + [pl.BlockSpec((8, width), lambda h: (0, 0))] * len(extra),
        out_specs=pl.BlockSpec((8, width), lambda h: (0, 0)),
        out_shape=jax.ShapeDtypeStruct((8, width), f32),
        scratch_shapes=[pltpu.VMEM((length, HEAD_DIM), bf16)] * 6,
        compiler_params=params(),
        cost_estimate=cost(24 * HEAD_DIM * work, 16 * length * heads * HEAD_DIM, 2 * work),
        name="teacher",
    )(timesteps, *arrays, *student_arrays, gains, out, lse, *extra)


def sum_kernel(n, groups, *refs):
    ins, out_ref = refs[:n], refs[n]
    parts = [ref[0:2, :] for ref in ins]
    while len(parts) > 1:
        parts = [parts[i] + parts[i + 1] for i in range(0, len(parts), 2)]
    for j in range(groups):
        out_ref[j, 0:2, :] = parts[0]
        out_ref[j, 2:, :] = ins[0][2:, :]


def clip_sum(parts, groups):
    rows, width = parts[0].shape
    return pl.pallas_call(
        functools.partial(sum_kernel, len(parts), groups),
        out_shape=jax.ShapeDtypeStruct((groups, rows, width), f32),
        name="clip_sum",
    )(*parts)


def final_kernel(groups, width, own, terms_ref, gain_ref, loss_ref, grad_ref, student_ref, ema_ref):
    loss = jnp.zeros((1, width), f32)
    for j in range(groups):
        cols = pl.ds(j * width, width)
        term = terms_ref[j, 0:2, :]
        loss = loss + terms_ref[j, 2:3, :]
        new = gain_ref[0:2, cols] - step_size * term
        ema_ref[:, cols] = ema_decay * gain_ref[2:4, cols] + (1.0 - ema_decay) * new
    loss_ref[0] = jnp.sum(loss)
    for z in range(groups * width // own):

        @pl.when(lax.axis_index("fsdp") == z)
        def _():
            for j in range(groups):
                low, high = max(j * width, z * own), min((j + 1) * width, (z + 1) * own)
                if low < high:
                    term = terms_ref[j, 0:2, low - j * width : high - j * width]
                    grad_ref[:, low - z * own : high - z * own] = term
                    student_ref[:, low - z * own : high - z * own] = gain_ref[0:2, low:high] - step_size * term


def finish(terms, gains, own):
    groups, _, width = terms.shape
    return pl.pallas_call(
        functools.partial(final_kernel, groups, width, own),
        out_shape=[
            jax.ShapeDtypeStruct((1,), f32),
            jax.ShapeDtypeStruct((2, own), f32),
            jax.ShapeDtypeStruct((2, own), f32),
            jax.ShapeDtypeStruct((2, groups * width), f32),
        ],
        out_specs=[pl.BlockSpec(memory_space=pltpu.SMEM)] + [pl.BlockSpec(memory_space=pltpu.VMEM)] * 3,
        name="finish",
    )(terms, gains)


def by_step(parts):
    return [parts[0]] + [swap(parts[step], "seq", step) for step in range(1, len(parts))]


def by_source(stacked):
    return [lax.all_to_all(stacked, "seq", split_axis=0, concat_axis=0, tiled=True)]


def local(
    query_teacher,
    key_teacher,
    value_teacher,
    query_student,
    key_student,
    value_student,
    timesteps,
    student_gain,
    ema_gain,
):
    groups = lax.axis_size("seq")
    clips = lax.axis_size("fsdp")
    tokens = query_teacher.shape[1]
    inner = query_teacher.shape[2]
    width = inner // groups
    heads = width // HEAD_DIM
    split = (heads + 1) // 2 * HEAD_DIM

    sent = prep(query_student[0], key_student[0], value_student[0], groups, width, [(0, width, True)])
    student_parts = by_step(sent)
    sent = prep(
        query_teacher[0],
        key_teacher[0],
        value_teacher[0],
        groups,
        width,
        [(0, split, False), (split, width - split, True)],
    )
    teacher_first = by_source(sent[0])
    gains = lax.all_gather(jnp.concatenate([student_gain, ema_gain], axis=0), "fsdp", axis=1, tiled=True)

    out, lse = student(student_parts, gains, groups, tokens, width)
    teacher_second = by_step(sent[1:])
    grads = teacher(
        timesteps, teacher_first, student_parts, gains, out, lse, None, 0, split // HEAD_DIM, groups, tokens, width
    )
    returned = by_source(out)[0]
    grads = teacher(
        timesteps,
        teacher_second,
        student_parts,
        gains,
        out,
        lse,
        grads,
        split // HEAD_DIM,
        heads - split // HEAD_DIM,
        groups,
        tokens,
        width,
    )
    student_out = jnp.moveaxis(returned, 0, 1).reshape(1, tokens, inner)
    terms = clip_sum([grads] + [swap(grads, "fsdp", step) for step in range(1, clips)], groups)
    terms = by_source(terms)[0]
    loss, gain_grad, new_student, new_ema = finish(terms, gains, student_gain.shape[1])
    return (student_out, loss, gain_grad, new_student, new_ema)


def solution(mesh):
    in_specs = (
        P("fsdp", "seq", None),
        P("fsdp", "seq", None),
        P("fsdp", "seq", None),
        P("fsdp", "seq", None),
        P("fsdp", "seq", None),
        P("fsdp", "seq", None),
        P("fsdp"),
        P(None, "fsdp"),
        P(None, "fsdp"),
    )
    out_specs = (P("fsdp", "seq", None), P("fsdp"), P(None, "fsdp"), P(None, "fsdp"), P())
    return jax.shard_map(local, mesh=mesh, in_specs=in_specs, out_specs=out_specs, check_vma=False)
```

profile of v0, /device:TPU:0, one launch (start us, length us, event | category | flops | bytes accessed | tf_op | source)
XLA Modules:
  0.0 145.8 jit_solution(14564309100484647793)
XLA Ops:
  0.6 1.2 copy-done
  1.9 1.2 copy-done.1
  3.1 1.2 copy-done.2
  4.3 2.6 %prep.3 = (bf16[8,3,128,256]{3,2,1,0:T(8,128)(2,1)}, bf16[3,128,256]{2,1,0:T(8,128)(2,1)S(1)}, bf16[3,128,256]{2,1,0:T(8,128)(2,1)}, bf16[3,128,256]{2,1,0:T(8,1...) custom-call(bf16[128,4096]{1,0:T(8,128)(2,1)S(1)} %bitcast.8, ...), custom_call_target="tpu_custom_call" | custom-call | flops 10485760 | bytes 6291456 | tf_op jit(solution)/shard_map/prep/pallas_call | solution.py:84
  8.9 5.3 %all-to-all-start.1 = ((bf16[8,3,128,256]{3,2,1,0:T(8,128)(2,1)}), bf16[8,3,128,256]{3,2,1,0:T(8,128)(2,1)S(1)}, u32[]{:S(2)}, u32[]{:S(2)}) async-start(bf16[8,3,128,256]{3,2,1,0:T(8,128)(2,1)} %get-tuple-element.46), calls=%async_computation.1 | async-start | bytes 3145728 | tf_op jit(solution)/shard_map/all_to_all | solution.py:322
  14.2 1.2 copy-done.4
  15.4 2.9 %prep.2 = (bf16[3,128,512]{2,1,0:T(8,128)(2,1)S(1)}, bf16[3,128,512]{2,1,0:T(8,128)(2,1)S(1)}, bf16[3,128,512]{2,1,0:T(8,128)(2,1)S(1)}, bf16[3,128,512]{2,1,0:T...) custom-call(bf16[128,4096]{1,0:T(8,128)(2,1)S(1)} %bitcast.11, ...), custom_call_target="tpu_custom_call" | custom-call | flops 10485760 | bytes 6291456 | tf_op jit(solution)/shard_map/prep/pallas_call | solution.py:84
  18.9 1.7 %collective-permute-start.1 = (bf16[3,128,512]{2,1,0:T(8,128)(2,1)S(1)}, bf16[3,128,512]{2,1,0:T(8,128)(2,1)S(1)}, u32[]{:S(2)}, u32[]{:S(2)}) collective-permute-start(bf16[3,128,512]{2,1,0:T(8,128)(2,1)S(1)} %get-tuple-element.30), channel_id=1, source_target_pairs={{0,2},{1,3},{2,0},{3,1},{4,6},{5,7},{6,4},{7,5},{8,10},{9,11},{10,... | collective-permute-start | bytes 1179656 | tf_op jit(solution)/shard_map/ppermute | solution.py:35
  20.6 1.7 %collective-permute-start.3 = (bf16[3,128,512]{2,1,0:T(8,128)(2,1)S(1)}, bf16[3,128,512]{2,1,0:T(8,128)(2,1)S(1)}, u32[]{:S(2)}, u32[]{:S(2)}) collective-permute-start(bf16[3,128,512]{2,1,0:T(8,128)(2,1)S(1)} %get-tuple-element.32), channel_id=1, source_target_pairs={{0,4},{1,5},{2,6},{3,7},{4,0},{5,1},{6,2},{7,3},{8,12},{9,13},{10,... | collective-permute-start | bytes 1179656 | tf_op jit(solution)/shard_map/ppermute | solution.py:35
  22.4 2.6 %collective-permute-start.5 = (bf16[3,128,512]{2,1,0:T(8,128)(2,1)S(1)}, bf16[3,128,512]{2,1,0:T(8,128)(2,1)S(1)}, u32[]{:S(2)}, u32[]{:S(2)}) collective-permute-start(bf16[3,128,512]{2,1,0:T(8,128)(2,1)S(1)} %get-tuple-element.34), channel_id=1, source_target_pairs={{0,6},{1,7},{2,4},{3,5},{4,2},{5,3},{6,0},{7,1},{8,14},{9,15},{10,... | collective-permute-start | bytes 1179656 | tf_op jit(solution)/shard_map/ppermute | solution.py:35
  25.0 18.3 %collective-permute-done.1.refs_2_.refs_4_.refs_11_ = bf16[3,128,512]{2,1,0:T(8,128)(2,1)S(1)} collective-permute-done((bf16[3,128,512]{2,1,0:T(8,128)(2,1)S(1)}, bf16[3,128,512]{2,1,0:T(8,128)(2,1)S(1)}, u32[]{:S(2)}, u32[]{:S(2)}) %collective-permute-start.1) | collective-permute-done | bytes 393248 | tf_op jit(solution)/shard_map/ppermute | solution.py:35
  44.2 13.4 %all_gather.3.refs_8_.refs_10_.refs_17_.gain_ref = f32[4,4096]{1,0:T(4,128)S(1)} all-gather(f32[4,1024]{1,0:T(4,128)S(1)} %pad_maximum_fusion), channel_id=1, replica_groups=mesh['fsdp'=4,'seq'=8] {'fsdp'}, dimensions={1}, use_global_device_ids=true | all-gather | bytes 81920 | tf_op jit(solution)/shard_map/all_gather | solution.py:355
  57.6 1.3 collective-permute-start.10
  59.0 1.8 %collective-permute-start.12 = (bf16[3,128,256]{2,1,0:T(8,128)(2,1)}, bf16[3,128,256]{2,1,0:T(8,128)(2,1)}, u32[]{:S(2)}, u32[]{:S(2)}) collective-permute-start(bf16[3,128,256]{2,1,0:T(8,128)(2,1)} %get-tuple-element.43), channel_id=1, source_target_pairs={{0,6},{1,7},{2,4},{3,5},{4,2},{5,3},{6,0},{7,1},{8,14},{9,15},{10,... | collective-permute-start | bytes 589832 | tf_op jit(solution)/shard_map/ppermute | solution.py:35
  61.1 1.0 collective-permute-start.13
  62.2 6.4 %collective-permute-done.6.refs_7_.refs_9_.refs_16_ = bf16[3,128,512]{2,1,0:T(8,128)(2,1)S(1)} collective-permute-done((bf16[3,128,512]{2,1,0:T(8,128)(2,1)S(1)}, bf16[3,128,512]{2,1,0:T(8,128)(2,1)S(1)}, u32[]{:S(2)}, u32[]{:S(2)}) %collective-permute-start.6) | collective-permute-done | bytes 393248 | tf_op jit(solution)/shard_map/ppermute | solution.py:35
  69.4 12.2 %student.1 = (bf16[8,128,512]{2,1,0:T(8,128)(2,1)}, f32[4,1024,128]{2,1,0:T(8,128)}) custom-call(bf16[3,128,512]{2,1,0:T(8,128)(2,1)S(1)} %get-tuple-element.28.refs_0_.refs_2_.refs_9_, bf16[3,128,512]{2,1,0:T(8,128)(2,1)S(1)} %collective-permute-done.refs_1_.refs_3_.refs_10_, bf16[3,128,512]{2,1,0:T(8,128)(2,1)S(1)} %collective-permute-done.1.refs_2_.refs_4_.refs_11_, ...), custom_call_target="tpu_custom_call" | custom-call | flops 4294967296 | bytes 4194304 | tf_op jit(solution)/shard_map/student/pallas_call | solution.py:151
  82.3 3.5 %collective-permute-done.11.refs_6_ = bf16[3,128,256]{2,1,0:T(8,128)(2,1)S(1)} collective-permute-done((bf16[3,128,256]{2,1,0:T(8,128)(2,1)S(1)}, bf16[3,128,256]{2,1,0:T(8,128)(2,1)S(1)}, u32[]{:S(2)}, u32[]{:S(2)}) %collective-permute-start.11) | collective-permute-done | bytes 196640 | tf_op jit(solution)/shard_map/ppermute | solution.py:35
  86.9 4.4 %all-to-all-start = ((bf16[8,128,512]{2,1,0:T(8,128)(2,1)}), bf16[8,128,512]{2,1,0:T(8,128)(2,1)}, u32[]{:S(2)}, u32[]{:S(2)}) async-start(bf16[8,128,512]{2,1,0:T(8,128)(2,1)} %get-tuple-element.36.refs_11_.refs_18_), calls=%async_computation | async-start | bytes 2097152 | tf_op jit(solution)/shard_map/all_to_all | solution.py:322
  92.3 1.0 copy-done.11
  95.4 13.3 %teacher.2.refs_20_ = f32[8,512]{1,0:T(8,128)S(1)} custom-call(s32[1]{0:T(128)S(6)} %copy.16.refs_0_, bf16[8,3,128,256]{3,2,1,0:T(8,128)(2,1)S(1)} %all-to-all-done.1.refs_1_, bf16[3,128,512]{2,1,0:T(8,128)(2,1)S(1)} %get-tuple-element.28.refs_0_.refs_2_.refs_9_, bf16[3,128,512]{2,1,0:T(8,128)(2,1)S(1)} %collective-permute-done.refs_1_.refs_3_.refs_10_, ...), custom_call_target="tpu_custom_call" | custom-call | flops 6442450944 | bytes 4194304 | tf_op jit(solution)/shard_map/teacher/pallas_call | solution.py:239
  108.8 13.2 %teacher.3.refs_0_ = f32[8,512]{1,0:T(8,128)S(1)} custom-call(s32[1]{0:T(128)S(6)} %copy.16.refs_0_, bf16[3,128,256]{2,1,0:T(8,128)(2,1)S(1)} %copy-done.20, bf16[3,128,256]{2,1,0:T(8,128)(2,1)} %collective-permute-done.7.refs_2_, bf16[3,128,256]{2,1,0:T(8,128)(2,1)} %collective-permute-done.8.refs_3_, bf16[3,128,256]{2,1,0:T(8,128)(2,1)} %collective-permute-done.9.refs_4_, ...), custom_call_target="tpu_custom_call" | custom-call | flops 6442450944 | bytes 4194304 | tf_op jit(solution)/shard_map/teacher/pallas_call | solution.py:239
  122.0 1.6 %collective-permute-start.14 = (f32[8,512]{1,0:T(8,128)S(1)}, f32[8,512]{1,0:T(8,128)S(1)}, u32[]{:S(2)}, u32[]{:S(2)}) collective-permute-start(f32[8,512]{1,0:T(8,128)S(1)} %teacher.3.refs_0_), channel_id=1, source_target_pairs={{0,8},{8,0},{16,24},{24,16},{1,9},{9,1},{17,25},{25,17},{2,10},{10... | collective-permute-start | bytes 49160 | tf_op jit(solution)/shard_map/ppermute | solution.py:35
  123.7 2.6 %collective-permute-start.15 = (f32[8,512]{1,0:T(8,128)S(1)}, f32[8,512]{1,0:T(8,128)S(1)}, u32[]{:S(2)}, u32[]{:S(2)}) collective-permute-start(f32[8,512]{1,0:T(8,128)S(1)} %teacher.3.refs_0_), channel_id=1, source_target_pairs={{0,16},{8,24},{16,0},{24,8},{1,17},{9,25},{17,1},{25,9},{2,18},{10... | collective-permute-start | bytes 49160 | tf_op jit(solution)/shard_map/ppermute | solution.py:35
  126.5 1.9 %collective-permute-done.15.refs_2_ = f32[8,512]{1,0:T(8,128)S(1)} collective-permute-done((f32[8,512]{1,0:T(8,128)S(1)}, f32[8,512]{1,0:T(8,128)S(1)}, u32[]{:S(2)}, u32[]{:S(2)}) %collective-permute-start.15) | collective-permute-done | bytes 16416 | tf_op jit(solution)/shard_map/ppermute | solution.py:35
  128.4 3.4 %collective-permute-done.16.refs_3_ = f32[8,512]{1,0:T(8,128)S(1)} collective-permute-done((f32[8,512]{1,0:T(8,128)S(1)}, f32[8,512]{1,0:T(8,128)S(1)}, u32[]{:S(2)}, u32[]{:S(2)}) %collective-permute-start.16) | collective-permute-done | bytes 16416 | tf_op jit(solution)/shard_map/ppermute | solution.py:35
  132.4 1.4 clip_sum.1
  133.9 3.9 %all-to-all-start.2 = ((f32[8,8,512]{2,1,0:T(8,128)}), f32[8,8,512]{2,1,0:T(8,128)S(1)}, u32[]{:S(2)}, u32[]{:S(2)}) async-start(f32[8,8,512]{2,1,0:T(8,128)} %clip_sum.1), calls=%async_computation.2 | async-start | bytes 262144 | tf_op jit(solution)/shard_map/all_to_all | solution.py:322
  137.8 1.6 %copy.14 = bf16[128,8,512]{0,2,1:T(8,128)(2,1)S(1)} copy(bf16[128,8,512]{2,0,1:T(8,128)(2,1)} %bitcast.3) | data formatting | bytes 2097152 | tf_op jit(solution)/shard_map/transpose | solution.py:377
  139.4 1.3 copy.15
  140.7 2.6 %all-to-all-done.2.terms_ref = f32[8,8,512]{2,1,0:T(8,128)S(1)} async-done(((f32[8,8,512]{2,1,0:T(8,128)}), f32[8,8,512]{2,1,0:T(8,128)S(1)}, u32[]{:S(2)}, u32[]{:S(2)}) %all-to-all-start.2) | async-done | bytes 131104 | tf_op jit(solution)/shard_map/all_to_all | solution.py:322
  144.0 1.7 %finish.1 = (f32[1]{0:T(128)}, f32[2,1024]{1,0:T(2,128)}, f32[2,1024]{1,0:T(2,128)}, f32[2,4096]{1,0:T(2,128)}) custom-call(f32[8,8,512]{2,1,0:T(8,128)} %copy-done.29, f32[4,4096]{1,0:T(4,128)} %copy-done.5), custom_call_target="tpu_custom_call" | custom-call | tf_op jit(solution)/shard_map/finish/pallas_call | solution.py:304
  (89 shorter events, 10.5 us)
Async XLA Ops:
  8.9 78.0 %all-to-all-start.1 = ((bf16[8,3,128,256]{3,2,1,0:T(8,128)(2,1)}), bf16[8,3,128,256]{3,2,1,0:T(8,128)(2,1)S(1)}, u32[]{:S(2)}, u32[]{:S(2)}) async-start(bf16[8,3,128,256]{3,2,1,0:T(8,128)(2,1)} %get-tuple-element.46), calls=%async_computation.1 | async-start | bytes 3145728 | tf_op jit(solution)/shard_map/all_to_all | solution.py:322
  15.4 28.7 %copy-start.33 = (f32[2,1024]{1,0:T(2,128)S(1)}, f32[2,1024]{1,0:T(2,128)}, u32[]{:S(2)}) copy-start(f32[2,1024]{1,0:T(2,128)} %param.17) | copy-start | bytes 24580
  15.4 28.7 %copy-start.34 = (f32[2,1024]{1,0:T(2,128)S(1)}, f32[2,1024]{1,0:T(2,128)}, u32[]{:S(2)}) copy-start(f32[2,1024]{1,0:T(2,128)} %param.16) | copy-start | bytes 24580
  15.4 42.2 %copy-start.24 = (bf16[3,128,256]{2,1,0:T(8,128)(2,1)S(1)}, bf16[3,128,256]{2,1,0:T(8,128)(2,1)}, u32[]{:S(2)}) copy-start(bf16[3,128,256]{2,1,0:T(8,128)(2,1)} %copy-done.23) | copy-start | bytes 589828
  15.4 43.5 %copy-start.22 = (bf16[3,128,256]{2,1,0:T(8,128)(2,1)S(1)}, bf16[3,128,256]{2,1,0:T(8,128)(2,1)}, u32[]{:S(2)}) copy-start(bf16[3,128,256]{2,1,0:T(8,128)(2,1)} %copy-done.21) | copy-start | bytes 589828
  18.3 4.1 %collective-permute-start = (bf16[3,128,512]{2,1,0:T(8,128)(2,1)S(1)}, bf16[3,128,512]{2,1,0:T(8,128)(2,1)S(1)}, u32[]{:S(2)}, u32[]{:S(2)}) collective-permute-start(bf16[3,128,512]{2,1,0:T(8,128)(2,1)S(1)} %get-tuple-element.29), channel_id=1, source_target_pairs={{0,1},{1,0},{2,3},{3,2},{4,5},{5,4},{6,7},{7,6},{8,9},{9,8},{10,11... | collective-permute-start | bytes 1179656 | tf_op jit(solution)/shard_map/ppermute | solution.py:35
  18.9 24.4 %collective-permute-start.1 = (bf16[3,128,512]{2,1,0:T(8,128)(2,1)S(1)}, bf16[3,128,512]{2,1,0:T(8,128)(2,1)S(1)}, u32[]{:S(2)}, u32[]{:S(2)}) collective-permute-start(bf16[3,128,512]{2,1,0:T(8,128)(2,1)S(1)} %get-tuple-element.30), channel_id=1, source_target_pairs={{0,2},{1,3},{2,0},{3,1},{4,6},{5,7},{6,4},{7,5},{8,10},{9,11},{10,... | collective-permute-start | bytes 1179656 | tf_op jit(solution)/shard_map/ppermute | solution.py:35
  20.6 37.0 %collective-permute-start.2 = (bf16[3,128,512]{2,1,0:T(8,128)(2,1)S(1)}, bf16[3,128,512]{2,1,0:T(8,128)(2,1)S(1)}, u32[]{:S(2)}, u32[]{:S(2)}) collective-permute-start(bf16[3,128,512]{2,1,0:T(8,128)(2,1)S(1)} %get-tuple-element.31), channel_id=1, source_target_pairs={{0,3},{1,2},{2,1},{3,0},{4,7},{5,6},{6,5},{7,4},{8,11},{9,10},{10,... | collective-permute-start | bytes 1179656 | tf_op jit(solution)/shard_map/ppermute | solution.py:35
  20.6 38.3 %collective-permute-start.3 = (bf16[3,128,512]{2,1,0:T(8,128)(2,1)S(1)}, bf16[3,128,512]{2,1,0:T(8,128)(2,1)S(1)}, u32[]{:S(2)}, u32[]{:S(2)}) collective-permute-start(bf16[3,128,512]{2,1,0:T(8,128)(2,1)S(1)} %get-tuple-element.32), channel_id=1, source_target_pairs={{0,4},{1,5},{2,6},{3,7},{4,0},{5,1},{6,2},{7,3},{8,12},{9,13},{10,... | collective-permute-start | bytes 1179656 | tf_op jit(solution)/shard_map/ppermute | solution.py:35
  22.3 36.7 %collective-permute-start.4 = (bf16[3,128,512]{2,1,0:T(8,128)(2,1)S(1)}, bf16[3,128,512]{2,1,0:T(8,128)(2,1)S(1)}, u32[]{:S(2)}, u32[]{:S(2)}) collective-permute-start(bf16[3,128,512]{2,1,0:T(8,128)(2,1)S(1)} %get-tuple-element.33), channel_id=1, source_target_pairs={{0,5},{1,4},{2,7},{3,6},{4,1},{5,0},{6,3},{7,2},{8,13},{9,12},{10,... | collective-permute-start | bytes 1179656 | tf_op jit(solution)/shard_map/ppermute | solution.py:35
  22.4 38.7 %collective-permute-start.5 = (bf16[3,128,512]{2,1,0:T(8,128)(2,1)S(1)}, bf16[3,128,512]{2,1,0:T(8,128)(2,1)S(1)}, u32[]{:S(2)}, u32[]{:S(2)}) collective-permute-start(bf16[3,128,512]{2,1,0:T(8,128)(2,1)S(1)} %get-tuple-element.34), channel_id=1, source_target_pairs={{0,6},{1,7},{2,4},{3,5},{4,2},{5,3},{6,0},{7,1},{8,14},{9,15},{10,... | collective-permute-start | bytes 1179656 | tf_op jit(solution)/shard_map/ppermute | solution.py:35
  43.3 25.3 %collective-permute-start.6 = (bf16[3,128,512]{2,1,0:T(8,128)(2,1)S(1)}, bf16[3,128,512]{2,1,0:T(8,128)(2,1)S(1)}, u32[]{:S(2)}, u32[]{:S(2)}) collective-permute-start(bf16[3,128,512]{2,1,0:T(8,128)(2,1)S(1)} %get-tuple-element.35), channel_id=1, source_target_pairs={{0,7},{1,6},{2,5},{3,4},{4,3},{5,2},{6,1},{7,0},{8,15},{9,14},{10,... | collective-permute-start | bytes 1179656 | tf_op jit(solution)/shard_map/ppermute | solution.py:35
  57.6 51.2 %copy-start.5 = (f32[4,4096]{1,0:T(4,128)}, f32[4,4096]{1,0:T(4,128)S(1)}, u32[]{:S(2)}) copy-start(f32[4,4096]{1,0:T(4,128)S(1)} %all_gather.3.refs_8_.refs_10_.refs_17_.gain_ref) | copy-start | bytes 196612
  57.6 24.1 %collective-permute-start.10 = (bf16[3,128,256]{2,1,0:T(8,128)(2,1)S(1)}, bf16[3,128,256]{2,1,0:T(8,128)(2,1)S(1)}, u32[]{:S(2)}, u32[]{:S(2)}) collective-permute-start(bf16[3,128,256]{2,1,0:T(8,128)(2,1)S(1)} %copy-done.24), channel_id=1, source_target_pairs={{0,4},{1,5},{2,6},{3,7},{4,0},{5,1},{6,2},{7,3},{8,12},{9,13},{10,... | collective-permute-start | bytes 589832 | tf_op jit(solution)/shard_map/ppermute | solution.py:35
  58.9 22.6 %copy-start.7 = (bf16[3,128,512]{2,1,0:T(8,128)(2,1)}, bf16[3,128,512]{2,1,0:T(8,128)(2,1)S(1)}, u32[]{:S(2)}) copy-start(bf16[3,128,512]{2,1,0:T(8,128)(2,1)S(1)} %collective-permute-done.3.refs_4_.refs_6_.refs_13_) | copy-start | bytes 1179652
  58.9 26.8 %collective-permute-start.11 = (bf16[3,128,256]{2,1,0:T(8,128)(2,1)S(1)}, bf16[3,128,256]{2,1,0:T(8,128)(2,1)S(1)}, u32[]{:S(2)}, u32[]{:S(2)}) collective-permute-start(bf16[3,128,256]{2,1,0:T(8,128)(2,1)S(1)} %copy-done.22), channel_id=1, source_target_pairs={{0,5},{1,4},{2,7},{3,6},{4,1},{5,0},{6,3},{7,2},{8,13},{9,12},{10,... | collective-permute-start | bytes 589832 | tf_op jit(solution)/shard_map/ppermute | solution.py:35
  59.0 22.6 %copy-start.10 = (bf16[3,128,512]{2,1,0:T(8,128)(2,1)}, bf16[3,128,512]{2,1,0:T(8,128)(2,1)S(1)}, u32[]{:S(2)}) copy-start(bf16[3,128,512]{2,1,0:T(8,128)(2,1)S(1)} %collective-permute-done.4.refs_5_.refs_7_.refs_14_) | copy-start | bytes 1179652
  59.0 49.7 %collective-permute-start.12 = (bf16[3,128,256]{2,1,0:T(8,128)(2,1)}, bf16[3,128,256]{2,1,0:T(8,128)(2,1)}, u32[]{:S(2)}, u32[]{:S(2)}) collective-permute-start(bf16[3,128,256]{2,1,0:T(8,128)(2,1)} %get-tuple-element.43), channel_id=1, source_target_pairs={{0,6},{1,7},{2,4},{3,5},{4,2},{5,3},{6,0},{7,1},{8,14},{9,15},{10,... | collective-permute-start | bytes 589832 | tf_op jit(solution)/shard_map/ppermute | solution.py:35
  61.1 20.5 %copy-start.13 = (bf16[3,128,512]{2,1,0:T(8,128)(2,1)}, bf16[3,128,512]{2,1,0:T(8,128)(2,1)S(1)}, u32[]{:S(2)}) copy-start(bf16[3,128,512]{2,1,0:T(8,128)(2,1)S(1)} %collective-permute-done.5.refs_6_.refs_8_.refs_15_) | copy-start | bytes 1179652
  61.1 47.6 %collective-permute-start.13 = (bf16[3,128,256]{2,1,0:T(8,128)(2,1)}, bf16[3,128,256]{2,1,0:T(8,128)(2,1)}, u32[]{:S(2)}, u32[]{:S(2)}) collective-permute-start(bf16[3,128,256]{2,1,0:T(8,128)(2,1)} %get-tuple-element.44), channel_id=1, source_target_pairs={{0,7},{1,6},{2,5},{3,4},{4,3},{5,2},{6,1},{7,0},{8,15},{9,14},{10,... | collective-permute-start | bytes 589832 | tf_op jit(solution)/shard_map/ppermute | solution.py:35
  68.6 40.1 %collective-permute-start.7 = (bf16[3,128,256]{2,1,0:T(8,128)(2,1)}, bf16[3,128,256]{2,1,0:T(8,128)(2,1)}, u32[]{:S(2)}, u32[]{:S(2)}) collective-permute-start(bf16[3,128,256]{2,1,0:T(8,128)(2,1)} %get-tuple-element.38), channel_id=1, source_target_pairs={{0,1},{1,0},{2,3},{3,2},{4,5},{5,4},{6,7},{7,6},{8,9},{9,8},{10,11... | collective-permute-start | bytes 589832 | tf_op jit(solution)/shard_map/ppermute | solution.py:35
  81.7 27.0 %collective-permute-start.8 = (bf16[3,128,256]{2,1,0:T(8,128)(2,1)}, bf16[3,128,256]{2,1,0:T(8,128)(2,1)}, u32[]{:S(2)}, u32[]{:S(2)}) collective-permute-start(bf16[3,128,256]{2,1,0:T(8,128)(2,1)} %get-tuple-element.39), channel_id=1, source_target_pairs={{0,2},{1,3},{2,0},{3,1},{4,6},{5,7},{6,4},{7,5},{8,10},{9,11},{10,... | collective-permute-start | bytes 589832 | tf_op jit(solution)/shard_map/ppermute | solution.py:35
  86.4 22.3 %collective-permute-start.9 = (bf16[3,128,256]{2,1,0:T(8,128)(2,1)}, bf16[3,128,256]{2,1,0:T(8,128)(2,1)}, u32[]{:S(2)}, u32[]{:S(2)}) collective-permute-start(bf16[3,128,256]{2,1,0:T(8,128)(2,1)} %get-tuple-element.40), channel_id=1, source_target_pairs={{0,3},{1,2},{2,1},{3,0},{4,7},{5,6},{6,5},{7,4},{8,11},{9,10},{10,... | collective-permute-start | bytes 589832 | tf_op jit(solution)/shard_map/ppermute | solution.py:35
  86.9 47.0 %all-to-all-start = ((bf16[8,128,512]{2,1,0:T(8,128)(2,1)}), bf16[8,128,512]{2,1,0:T(8,128)(2,1)}, u32[]{:S(2)}, u32[]{:S(2)}) async-start(bf16[8,128,512]{2,1,0:T(8,128)(2,1)} %get-tuple-element.36.refs_11_.refs_18_), calls=%async_computation | async-start | bytes 2097152 | tf_op jit(solution)/shard_map/all_to_all | solution.py:322
  95.3 13.5 %copy-start.18 = (bf16[3,128,512]{2,1,0:T(8,128)(2,1)S(1)}, bf16[3,128,512]{2,1,0:T(8,128)(2,1)}, u32[]{:S(2)}) copy-start(bf16[3,128,512]{2,1,0:T(8,128)(2,1)} %copy-done.16) | copy-start | bytes 1179652
  95.3 13.5 %copy-start.20 = (bf16[3,128,256]{2,1,0:T(8,128)(2,1)S(1)}, bf16[3,128,256]{2,1,0:T(8,128)(2,1)}, u32[]{:S(2)}) copy-start(bf16[3,128,256]{2,1,0:T(8,128)(2,1)} %copy-done.19) | copy-start | bytes 589828
  95.3 13.5 %copy-start.26 = (bf16[3,128,256]{2,1,0:T(8,128)(2,1)S(1)}, bf16[3,128,256]{2,1,0:T(8,128)(2,1)}, u32[]{:S(2)}) copy-start(bf16[3,128,256]{2,1,0:T(8,128)(2,1)} %copy-done.25) | copy-start | bytes 589828
  95.4 13.5 %copy-start.28 = (bf16[3,128,256]{2,1,0:T(8,128)(2,1)S(1)}, bf16[3,128,256]{2,1,0:T(8,128)(2,1)}, u32[]{:S(2)}) copy-start(bf16[3,128,256]{2,1,0:T(8,128)(2,1)} %copy-done.27) | copy-start | bytes 589828
  122.0 4.5 %collective-permute-start.14 = (f32[8,512]{1,0:T(8,128)S(1)}, f32[8,512]{1,0:T(8,128)S(1)}, u32[]{:S(2)}, u32[]{:S(2)}) collective-permute-start(f32[8,512]{1,0:T(8,128)S(1)} %teacher.3.refs_0_), channel_id=1, source_target_pairs={{0,8},{8,0},{16,24},{24,16},{1,9},{9,1},{17,25},{25,17},{2,10},{10... | collective-permute-start | bytes 49160 | tf_op jit(solution)/shard_map/ppermute | solution.py:35
  123.7 4.7 %collective-permute-start.15 = (f32[8,512]{1,0:T(8,128)S(1)}, f32[8,512]{1,0:T(8,128)S(1)}, u32[]{:S(2)}, u32[]{:S(2)}) collective-permute-start(f32[8,512]{1,0:T(8,128)S(1)} %teacher.3.refs_0_), channel_id=1, source_target_pairs={{0,16},{8,24},{16,0},{24,8},{1,17},{9,25},{17,1},{25,9},{2,18},{10... | collective-permute-start | bytes 49160 | tf_op jit(solution)/shard_map/ppermute | solution.py:35
  126.3 5.5 %collective-permute-start.16 = (f32[8,512]{1,0:T(8,128)S(1)}, f32[8,512]{1,0:T(8,128)S(1)}, u32[]{:S(2)}, u32[]{:S(2)}) collective-permute-start(f32[8,512]{1,0:T(8,128)S(1)} %teacher.3.refs_0_), channel_id=1, source_target_pairs={{0,24},{8,16},{16,8},{24,0},{1,25},{9,17},{17,9},{25,1},{2,26},{10... | collective-permute-start | bytes 49160 | tf_op jit(solution)/shard_map/ppermute | solution.py:35
  133.9 9.4 %all-to-all-start.2 = ((f32[8,8,512]{2,1,0:T(8,128)}), f32[8,8,512]{2,1,0:T(8,128)S(1)}, u32[]{:S(2)}, u32[]{:S(2)}) async-start(f32[8,8,512]{2,1,0:T(8,128)} %clip_sum.1), calls=%async_computation.2 | async-start | bytes 262144 | tf_op jit(solution)/shard_map/all_to_all | solution.py:322
  (23 other events, 99.7 us)
where the time goes:
time: 147 us; the launch traced here: 146 us
  Pallas kernels  47.3 us (32%)
  waiting for transfers between devices  36.6 us (25%)
  starting transfers between devices  30.9 us (21%)
  local copies, waits for them, and re-layouts  15.8 us (11%)
  blocking collectives  13.4 us (9%)
  between operations  1.77 us (1%)
    ppermute x17, waiting for transfers between devices, swap(): return lax.ppermute(x, axis, [(i, i ^ step) for i in range(size)])  34 us
    pallas_call x2, Pallas kernels, teacher(): pl.pallas_call(functools.partial(teacher_kernel, groups, tokens, width, f...  26.5 us
    ppermute x17, starting transfers between devices, swap(): return lax.ppermute(x, axis, [(i, i ^ step) for i in range(size)])  17.3 us
    unnamed x71, local copies, waits for them, and re-layouts  14.2 us
    all_to_all x3, starting transfers between devices, by_source(): lax.all_to_all(stacked, 'seq', split_axis=0, concat_axis=0, tiled=True)  13.6 us
    all_gather x1, blocking collectives, local(): lax.all_gather(jnp.concatenate([student_gain, ema_gain], axis=0), 'fsdp',...  13.4 us
    pallas_call x1, Pallas kernels, student(): pl.pallas_call(functools.partial(student_kernel, groups, tokens, width, l...  12.2 us
    pallas_call x2, Pallas kernels, prep(): pl.pallas_call(functools.partial(prep_kernel, groups, width, plans), grid...  5.44 us
  transfers between devices with their start and end apart: 20, of which 8 were waited for; matrix products, arithmetic and copies ran while one was open for 2% of the time, Pallas kernels for 30%

commit v1 on v0

v1 whole, which is shorter than its diff:
```python
import functools
import math

import jax
import jax.numpy as jnp
from jax import lax
from jax.experimental import pallas as pl
from jax.experimental.pallas import tpu as pltpu
from jax.sharding import PartitionSpec as P

HEAD_DIM = 128
TSTEPS = 50

norm_eps = 1e-06
step_size = 0.01
ema_decay = 0.95

VMEM_BYTES = 60 * 1024 * 1024
STUDENT_BLOCK = 512
TEACHER_BLOCK = 512
TERMS = 4

f32 = jnp.float32
bf16 = jnp.bfloat16


def params(limit=VMEM_BYTES):
    return pltpu.CompilerParams(vmem_limit_bytes=limit)


def cost(flops, nbytes, exps=0):
    return pl.CostEstimate(flops=flops, bytes_accessed=nbytes, transcendentals=exps)


def swap(x, axis, step):
    size = lax.axis_size(axis)
    return lax.ppermute(x, axis, [(i, i ^ step) for i in range(size)])


def nn(a, b):
    return lax.dot_general(a, b, (((1,), (0,)), ((), ())), preferred_element_type=f32)


def prep_kernel(groups, width, plans, *refs):
    ins, outs = refs[:3], refs[3:]
    me = lax.axis_index("seq")
    inverse = []
    for x_ref in ins[:2]:
        wide = x_ref[...].astype(f32)
        inverse.append(lax.rsqrt(jnp.mean(wide * wide, axis=-1, keepdims=True) + norm_eps))

    at = 0
    for first, columns, by_step in plans:
        for slot in range(groups):
            if by_step:
                col = pl.multiple_of((me ^ slot) * width + first, HEAD_DIM)
            else:
                col = slot * width + first
            for a in range(3):
                part = ins[a][:, pl.ds(col, columns)]
                if a < 2:
                    part = (part.astype(f32) * inverse[a]).astype(bf16)
                for h in range(columns // HEAD_DIM):
                    head = part[:, h * HEAD_DIM : (h + 1) * HEAD_DIM]
                    if by_step:
                        outs[at + slot][h, a] = head
                    else:
                        outs[at][slot, h, a] = head
        at += groups if by_step else 1


def prep(q, k, v, groups, width, plans):
    tokens, inner = q.shape
    rows = min(32, tokens)
    shapes, specs = [], []
    for _, columns, by_step in plans:
        heads = columns // HEAD_DIM
        if by_step:
            for _ in range(groups):
                shapes.append(jax.ShapeDtypeStruct((heads, 3, tokens, HEAD_DIM), bf16))
                specs.append(pl.BlockSpec((heads, 3, rows, HEAD_DIM), lambda i: (0, 0, i, 0)))
        else:
            shapes.append(jax.ShapeDtypeStruct((groups, heads, 3, tokens, HEAD_DIM), bf16))
            specs.append(pl.BlockSpec((groups, heads, 3, rows, HEAD_DIM), lambda i: (0, 0, 0, i, 0)))
    return pl.pallas_call(
        functools.partial(prep_kernel, groups, width, plans),
        grid=(tokens // rows,),
        in_specs=[pl.BlockSpec((rows, inner), lambda i: (i, 0))] * 3,
        out_specs=specs,
        out_shape=shapes,
        compiler_params=params(),
        cost_estimate=cost(20 * tokens * inner, 12 * tokens * inner),
        name="prep",
    )(q, k, v)


def scales(refs):
    found = []
    for x_ref in refs:
        wide = x_ref[...].astype(f32)
        found.append(lax.rsqrt(jnp.mean(wide * wide, axis=-1, keepdims=True) + norm_eps))
    return found


def unit_part(ins, inverse, a, col):
    part = ins[a][:, pl.ds(col, HEAD_DIM)]
    return (part.astype(f32) * inverse[a]).astype(bf16) if a < 2 else part


def sibling_kernel(groups, width, *refs):
    ins, out_ref = refs[:3], refs[3]
    me = lax.axis_index("seq")
    inverse = scales(ins[:2])
    for pair in range(groups // 2):
        for h in range(width // HEAD_DIM):
            col = pl.multiple_of((me ^ (2 * pair + 1)) * width + h * HEAD_DIM, HEAD_DIM)
            for a in range(3):
                out_ref[pair, h, a] = unit_part(ins, inverse, a, col)


def pair_kernel(groups, width, counts, *refs):
    ins, near_ref, outs = refs[:3], refs[3], refs[4:]
    me = lax.axis_index("seq")
    inverse = scales(ins[:2])
    at = first = 0
    for count in counts:
        for pair in range(groups // 2):
            for h in range(count):
                col = pl.multiple_of((me ^ (2 * pair)) * width + (first + h) * HEAD_DIM, HEAD_DIM)
                for a in range(3):
                    outs[at + pair][0, h, a] = unit_part(ins, inverse, a, col)
                    outs[at + pair][1, h, a] = near_ref[pair, first + h, a]
        at += groups // 2
        first += count


def prep_pairs(q, k, v, groups, width, counts, near):
    tokens, inner = q.shape
    heads = width // HEAD_DIM
    rows = min(32, tokens)
    in_specs = [pl.BlockSpec((rows, inner), lambda i: (i, 0))] * 3
    near_spec = pl.BlockSpec((groups // 2, heads, 3, rows, HEAD_DIM), lambda i: (0, 0, 0, i, 0))
    near_shape = jax.ShapeDtypeStruct((groups // 2, heads, 3, tokens, HEAD_DIM), bf16)
    if near is None:
        return pl.pallas_call(
            functools.partial(sibling_kernel, groups, width),
            grid=(tokens // rows,),
            in_specs=in_specs,
            out_specs=near_spec,
            out_shape=near_shape,
            compiler_params=params(),
            cost_estimate=cost(20 * tokens * inner, 9 * tokens * inner),
            name="prep_near",
        )(q, k, v)
    shapes, specs = [], []
    for count in counts:
        for _ in range(groups // 2):
            shapes.append(jax.ShapeDtypeStruct((2, count, 3, tokens, HEAD_DIM), bf16))
            specs.append(pl.BlockSpec((2, count, 3, rows, HEAD_DIM), lambda i: (0, 0, 0, i, 0)))
    return pl.pallas_call(
        functools.partial(pair_kernel, groups, width, counts),
        grid=(tokens // rows,),
        in_specs=in_specs + [near_spec],
        out_specs=specs,
        out_shape=shapes,
        compiler_params=params(),
        cost_estimate=cost(20 * tokens * inner, 15 * tokens * inner),
        name="prep_pairs",
    )(q, k, v, near)


def part_at(refs, me, slot, a):
    if refs[0].ndim == 5:
        return refs[slot // 2][slot % 2, 0, a]
    return refs[slot][0, a]


def head_gains(gain_ref, me, width, column):
    own = gain_ref.shape[2]
    tile = (me * width + column) // HEAD_DIM
    tiles = own // HEAD_DIM
    col = pl.multiple_of(lax.rem(tile, tiles) * HEAD_DIM, HEAD_DIM)
    return gain_ref[tile // tiles, :, pl.ds(col, HEAD_DIM)]


def with_gain(unit, gain):
    return (unit.astype(f32) * gain).astype(bf16)


def nt(a, b):
    return lax.dot_general(a, b, (((1,), (1,)), ((), ())), preferred_element_type=f32)


def load(refs, me, groups, tokens, gains, q_scr, k_scr, v_scr):
    for slot in range(groups):
        rows = pl.ds(slot * tokens, tokens)
        q_scr[rows, :] = with_gain(part_at(refs, me, slot, 0), gains[0])
        k_scr[rows, :] = with_gain(part_at(refs, me, slot, 1), gains[1])
        v_scr[rows, :] = part_at(refs, me, slot, 2)


def probabilities(scores):
    factor = HEAD_DIM ** (-0.5) * math.log2(math.e)
    top = jnp.max(scores, axis=-1, keepdims=True)
    raised = jnp.exp2((scores - top) * factor)
    total = jnp.sum(raised, axis=-1, keepdims=True)
    return raised * (1.0 / total), top * factor + jnp.log2(total)


def student_kernel(groups, tokens, width, n_in, *refs):
    ins = refs[:n_in]
    gain_ref, out_ref, lse_ref, q_scr, k_scr, v_scr = refs[n_in:]
    me = lax.axis_index("seq")
    gains = head_gains(gain_ref, me, width, pl.program_id(0) * HEAD_DIM)
    load(ins, me, groups, tokens, (gains[0:1], gains[1:2]), q_scr, k_scr, v_scr)
    length = groups * tokens
    block = min(STUDENT_BLOCK, length)
    scores = nt(q_scr[0:block, :], k_scr[...])
    for start in range(0, length, block):
        rows = pl.ds(start, block)
        later = start + block
        following = nt(q_scr[later : later + block, :], k_scr[...]) if later < length else None
        probs, lse = probabilities(scores)
        scores = following
        out = nn(probs.astype(bf16), v_scr[...]).astype(bf16)
        lse_ref[0, rows, :] = jnp.broadcast_to(lse, (block, HEAD_DIM))
        for j in range(block // tokens):
            out_ref[me ^ (start // tokens + j), 0] = out[j * tokens : (j + 1) * tokens]


def chunk_specs(arrays, groups, tokens, first):
    if arrays[0].ndim == 5:
        return [pl.BlockSpec((2, 1, 3, tokens, HEAD_DIM), lambda h: (0, first + h, 0, 0, 0))] * len(arrays)
    return [pl.BlockSpec((1, 3, tokens, HEAD_DIM), lambda h: (first + h, 0, 0, 0))] * groups


def student(arrays, gains, groups, tokens, width):
    heads = width // HEAD_DIM
    length = groups * tokens
    work = length * length * heads
    return pl.pallas_call(
        functools.partial(student_kernel, groups, tokens, width, len(arrays)),
        grid=(heads,),
        in_specs=chunk_specs(arrays, groups, tokens, 0) + [pl.BlockSpec(gains.shape, lambda h: (0, 0, 0))],
        out_specs=[
            pl.BlockSpec((groups, 1, tokens, HEAD_DIM), lambda h: (0, h, 0, 0)),
            pl.BlockSpec((1, length, HEAD_DIM), lambda h: (h, 0, 0)),
        ],
        out_shape=[
            jax.ShapeDtypeStruct((groups, heads, tokens, HEAD_DIM), bf16),
            jax.ShapeDtypeStruct((heads, length, HEAD_DIM), f32),
        ],
        scratch_shapes=[pltpu.VMEM((length, HEAD_DIM), bf16)] * 3,
        compiler_params=params(),
        cost_estimate=cost(8 * HEAD_DIM * work, 8 * length * width, work),
        name="student",
    )(*arrays, gains)


def teacher_kernel(groups, tokens, width, first, n_teacher, n_student, has_before, *refs):
    step_ref, *refs = refs
    teacher_refs, refs = refs[:n_teacher], refs[n_teacher:]
    student_refs, refs = refs[:n_student], refs[n_student:]
    gain_ref, out_ref, lse_ref, *refs = refs
    if has_before:
        before_ref, *refs = refs
    all_ref, grad_ref, qt, kt, vt, qs, ks, vs = refs
    length = groups * tokens
    block = min(TEACHER_BLOCK, length)
    scale = HEAD_DIM ** (-0.5)
    factor = scale * math.log2(math.e)
    head = pl.program_id(0)
    me = lax.axis_index("seq")
    column = (first + head) * HEAD_DIM
    gains = head_gains(gain_ref, me, width, column)
    load(teacher_refs, me, groups, tokens, (gains[2:3], gains[3:4]), qt, kt, vt)
    load(student_refs, me, groups, tokens, (gains[0:1], gains[1:2]), qs, ks, vs)
    step = jnp.full((1, HEAD_DIM), step_ref[0], jnp.int32).astype(f32)
    weight = 1.0 / (0.05 + (step + 1.0) / TSTEPS)
    share = weight / (length * (groups * width // HEAD_DIM))

    @pl.when(head == 0)
    def _():
        grad_ref[...] = before_ref[...] if has_before else jnp.zeros_like(grad_ref)

    squares = jnp.zeros((1, HEAD_DIM), f32)
    term_q = jnp.zeros((1, HEAD_DIM), f32)
    key_grad = None
    for start in range(0, length, block):
        rows = pl.ds(start, block)
        slots = range(start // tokens, start // tokens + block // tokens)
        scores = nt(qt[rows, :], kt[...])
        student_scores = nt(qs[rows, :], ks[...])
        probs, _ = probabilities(scores)
        target = nn(probs.astype(bf16), vt[...]).astype(bf16)
        out = jnp.concatenate([out_ref[me ^ slot, 0] for slot in slots], axis=0)
        diff = out.astype(f32) - target.astype(f32)
        squares = squares + jnp.sum(diff * diff, axis=0, keepdims=True)
        error = (2.0 * share * diff).astype(bf16)
        dprob = nt(error, vs[...])
        lse = jnp.concatenate([lse_ref[0, rows, :]] * (length // HEAD_DIM), axis=1)
        probs = jnp.exp2(student_scores * factor - lse)
        inner = jnp.sum(probs * dprob, axis=-1, keepdims=True)
        dscore = (probs * (dprob - inner)).astype(bf16)
        dquery = (nn(dscore, ks[...]) * scale).astype(bf16)
        unit = jnp.concatenate([part_at(student_refs, me, slot, 0) for slot in slots], axis=0)
        term_q = term_q + jnp.sum(dquery.astype(f32) * unit.astype(f32), axis=0, keepdims=True)
        part = nn(jnp.transpose(qs[rows, :]), dscore)
        key_grad = part if key_grad is None else key_grad + part
    dkey = (jnp.transpose(key_grad) * scale).astype(bf16)
    unit = jnp.concatenate([part_at(student_refs, me, slot, 1) for slot in range(groups)], axis=0)
    term_k = jnp.sum(dkey.astype(f32) * unit.astype(f32), axis=0, keepdims=True)
    cols = pl.ds(pl.multiple_of(column, HEAD_DIM), HEAD_DIM)
    grad_ref[0:1, cols] = term_q
    grad_ref[1:2, cols] = term_k
    grad_ref[2:3, cols] = share * squares

    @pl.when(head == pl.num_programs(0) - 1)
    def _():
        for copy in range(all_ref.shape[0]):
            all_ref[copy] = grad_ref[...]


def teacher(timesteps, arrays, student_arrays, gains, out, lse, before, first, heads, groups, tokens, width, copies):
    length = groups * tokens
    work = length * length * heads
    extra = [] if before is None else [before]
    return pl.pallas_call(
        functools.partial(
            teacher_kernel, groups, tokens, width, first, len(arrays), len(student_arrays), before is not None
        ),
        grid=(heads,),
        in_specs=[pl.BlockSpec(memory_space=pltpu.SMEM)]
        + chunk_specs(arrays, groups, tokens, 0)
        + chunk_specs(student_arrays, groups, tokens, first)
        + [
            pl.BlockSpec(gains.shape, lambda h: (0, 0, 0)),
            pl.BlockSpec((groups, 1, tokens, HEAD_DIM), lambda h: (0, first + h, 0, 0)),
            pl.BlockSpec((1, length, HEAD_DIM), lambda h: (first + h, 0, 0)),
        ]
        + [pl.BlockSpec((None, TERMS, width), lambda h: (0, 0, 0))] * len(extra),
        out_specs=pl.BlockSpec((copies, TERMS, width), lambda h: (0, 0, 0)),
        out_shape=jax.ShapeDtypeStruct((copies, TERMS, width), f32),
        scratch_shapes=[pltpu.VMEM((TERMS, width), f32)] + [pltpu.VMEM((length, HEAD_DIM), bf16)] * 6,
        compiler_params=params(),
        cost_estimate=cost(24 * HEAD_DIM * work, 16 * length * heads * HEAD_DIM, 2 * work),
        name="teacher",
    )(timesteps, *arrays, *student_arrays, gains, out, lse, *extra)


def final_kernel(clips, groups, width, own, terms_ref, gain_ref, loss_ref, grad_ref, student_ref, ema_ref):
    clip = lax.axis_index("fsdp")
    loss = jnp.zeros((1, width), f32)
    terms = []
    for j in range(groups):
        term = terms_ref[j, 0:2, :]
        for other in range(1, clips):
            term = term + terms_ref[other * groups + j, 0:2, :]
        terms.append(term)
        loss = loss + terms_ref[clip * groups + j, 2:3, :]
    loss_ref[0] = jnp.sum(loss)
    for z in range(clips):
        pieces = []
        for j in range(groups):
            low, high = max(j * width, z * own), min((j + 1) * width, (z + 1) * own)
            if low < high:
                pieces.append(terms[j][:, low - j * width : high - j * width])
        term = jnp.concatenate(pieces, axis=1)
        new = gain_ref[z, 0:2, :] - step_size * term
        ema_ref[:, z * own : (z + 1) * own] = ema_decay * gain_ref[z, 2:4, :] + (1.0 - ema_decay) * new

        @pl.when(clip == z)
        def _():
            grad_ref[...] = term
            student_ref[...] = new


def finish(terms, gains, groups, own):
    devices, _, width = terms.shape
    return pl.pallas_call(
        functools.partial(final_kernel, devices // groups, groups, width, own),
        out_shape=[
            jax.ShapeDtypeStruct((1,), f32),
            jax.ShapeDtypeStruct((2, own), f32),
            jax.ShapeDtypeStruct((2, own), f32),
            jax.ShapeDtypeStruct((2, groups * width), f32),
        ],
        out_specs=[pl.BlockSpec(memory_space=pltpu.SMEM)] + [pl.BlockSpec(memory_space=pltpu.VMEM)] * 3,
        name="finish",
    )(terms, gains)


def assemble_kernel(parts_ref, out_ref):
    groups, heads = parts_ref.shape[:2]
    for j in range(groups):
        for h in range(heads):
            at = (j * heads + h) * HEAD_DIM
            out_ref[0, :, at : at + HEAD_DIM] = parts_ref[j, h]


def assemble(parts):
    groups, heads, tokens, _ = parts.shape
    rows = min(32, tokens)
    return pl.pallas_call(
        assemble_kernel,
        grid=(tokens // rows,),
        in_specs=[pl.BlockSpec((groups, heads, rows, HEAD_DIM), lambda i: (0, 0, i, 0))],
        out_specs=pl.BlockSpec((1, rows, groups * heads * HEAD_DIM), lambda i: (0, i, 0)),
        out_shape=jax.ShapeDtypeStruct((1, tokens, groups * heads * HEAD_DIM), parts.dtype),
        compiler_params=params(),
        name="assemble",
    )(parts)


def by_step(parts):
    size = len(parts)
    received = list(parts)
    for step in [*range(2, size, 2), *range(3, size, 2), 1]:
        received[step] = swap(parts[step], "seq", step)
    return received


def by_pairs(parts):
    return [parts[0]] + [swap(parts[pair], "seq", 2 * pair) for pair in range(1, len(parts))]


def by_source(stacked):
    return [lax.all_to_all(stacked, "seq", split_axis=0, concat_axis=0, tiled=True)]


def local(
    query_teacher,
    key_teacher,
    value_teacher,
    query_student,
    key_student,
    value_student,
    timesteps,
    student_gain,
    ema_gain,
):
    groups = lax.axis_size("seq")
    clips = lax.axis_size("fsdp")
    tokens = query_teacher.shape[1]
    inner = query_teacher.shape[2]
    width = inner // groups
    heads = width // HEAD_DIM
    split = max(heads - 1, 1) * HEAD_DIM

    sent = prep(query_student[0], key_student[0], value_student[0], groups, width, [(0, width, True)])
    student_parts = by_step(sent)
    sent, later = lax.optimization_barrier((sent, (query_teacher, key_teacher, value_teacher)))
    later = [x[0] for x in later]
    counts = (split // HEAD_DIM, heads - split // HEAD_DIM)
    near = prep_pairs(*later, groups, width, counts, None)
    near, own_gains = lax.optimization_barrier((near, jnp.concatenate([student_gain, ema_gain], axis=0)))
    own_gains = jnp.broadcast_to(own_gains, (clips, *own_gains.shape))
    gains = lax.all_to_all(own_gains, "fsdp", split_axis=0, concat_axis=0, tiled=True)
    near, gains = lax.optimization_barrier((swap(near, "seq", 1), gains))
    sent = prep_pairs(*later, groups, width, counts, near)
    first_sent, second_sent = sent[: groups // 2], sent[groups // 2 :]
    teacher_first = by_pairs(first_sent)
    student_parts, second_sent = lax.optimization_barrier((student_parts, second_sent))
    teacher_second = by_pairs(second_sent)
    out, lse = student(student_parts, gains, groups, tokens, width)
    teacher_first, going = lax.optimization_barrier((teacher_first, out))
    returned = by_source(going)[0]
    grads = teacher(
        timesteps, teacher_first, student_parts, gains, out, lse, None, 0, split // HEAD_DIM, groups, tokens, width, 1
    )
    grads = teacher(
        timesteps,
        teacher_second,
        student_parts,
        gains,
        out,
        lse,
        grads,
        split // HEAD_DIM,
        heads - split // HEAD_DIM,
        groups,
        tokens,
        width,
        clips * groups,
    )
    returned, grads = lax.optimization_barrier((returned, grads))
    student_out = assemble(returned)
    terms = lax.all_to_all(grads, ("fsdp", "seq"), split_axis=0, concat_axis=0, tiled=True)
    loss, gain_grad, new_student, new_ema = finish(terms, gains, groups, student_gain.shape[1])
    return (student_out, loss, gain_grad, new_student, new_ema)


def solution(mesh):
    in_specs = (
        P("fsdp", "seq", None),
        P("fsdp", "seq", None),
        P("fsdp", "seq", None),
        P("fsdp", "seq", None),
        P("fsdp", "seq", None),
        P("fsdp", "seq", None),
        P("fsdp"),
        P(None, "fsdp"),
        P(None, "fsdp"),
    )
    out_specs = (P("fsdp", "seq", None), P("fsdp"), P(None, "fsdp"), P(None, "fsdp"), P())
    return jax.shard_map(local, mesh=mesh, in_specs=in_specs, out_specs=out_specs, check_vma=False)
```

time: 147 us -> 126 us (0.86)
  local copies, waits for them, and re-layouts: 15.8 us -> 3.74 us
  waiting for transfers between devices: 36.6 us -> 27.6 us
  Pallas kernels: 47.3 us -> 54.4 us
  starting transfers between devices: 30.9 us -> 27.1 us
  blocking collectives: 13.4 us -> 10.5 us
    ppermute x17 -> x14, waiting for transfers between devices: 34 us -> 20.4 us  [swap(): return lax.ppermute(x, axis, [(i, i ^ step) for i in range(size)])]
    all_gather x1 -> x0, blocking collectives: 13.4 us -> none  [local(): lax.all_gather(jnp.concatenate([student_gain, ema_gain], axis=0), 'fsdp',...]
    pallas_call x2 -> x4, Pallas kernels: 3.15 us -> 14.6 us  [the longest x1 5.05 us: prep_pairs(): pl.pallas_call(functools.partial(pair_kernel, groups, width, counts), gri...]
    all_to_all x0 -> x1, blocking collectives: none -> 10.5 us  [local(): lax.all_to_all(own_gains, 'fsdp', split_axis=0, concat_axis=0, tiled=True)]
    unnamed x71 -> x34, local copies, waits for them, and re-layouts: 14.2 us -> 3.73 us
    all_to_all x3 -> x1, starting transfers between devices: 13.6 us -> 3.75 us  [by_source(): lax.all_to_all(stacked, 'seq', split_axis=0, concat_axis=0, tiled=True)]
    all_to_all x0 -> x1, waiting for transfers between devices: none -> 7.15 us  [local(): lax.all_to_all(grads, ('fsdp', 'seq'), split_axis=0, concat_axis=0, tiled...]
    all_to_all x0 -> x1, starting transfers between devices: none -> 6.29 us  [local(): lax.all_to_all(grads, ('fsdp', 'seq'), split_axis=0, concat_axis=0, tiled...]
  transfers between devices with their start and end apart: 20 -> 16, of which waited for: 8 -> 4; matrix products, arithmetic and copies ran while one was open for 2% -> 0% of each run, Pallas kernels for 30% -> 35%
where the time goes in v1:
time: 126 us; the launch traced here: 125 us
  Pallas kernels  54.4 us (43%)
  waiting for transfers between devices  27.6 us (22%)
  starting transfers between devices  27.1 us (22%)
  blocking collectives  10.5 us (8%)
  local copies, waits for them, and re-layouts  3.74 us (3%)
  between operations  1.68 us (1%)
    pallas_call x2, Pallas kernels, teacher(): pl.pallas_call(functools.partial(teacher_kernel, groups, tokens, width, f...  25.2 us
    ppermute x14, waiting for transfers between devices, swap(): return lax.ppermute(x, axis, [(i, i ^ step) for i in range(size)])  20.4 us
    ppermute x14, starting transfers between devices, swap(): return lax.ppermute(x, axis, [(i, i ^ step) for i in range(size)])  17.1 us
    all_to_all x1, blocking collectives, local(): lax.all_to_all(own_gains, 'fsdp', split_axis=0, concat_axis=0, tiled=True)  10.5 us
    pallas_call x1, Pallas kernels, student(): pl.pallas_call(functools.partial(student_kernel, groups, tokens, width, l...  10.1 us
    all_to_all x1, waiting for transfers between devices, local(): lax.all_to_all(grads, ('fsdp', 'seq'), split_axis=0, concat_axis=0, tiled...  7.15 us
    all_to_all x1, starting transfers between devices, local(): lax.all_to_all(grads, ('fsdp', 'seq'), split_axis=0, concat_axis=0, tiled...  6.29 us
    pallas_call x1, Pallas kernels, prep_pairs(): pl.pallas_call(functools.partial(pair_kernel, groups, width, counts), gri...  5.05 us
  transfers between devices with their start and end apart: 16, of which 4 were waited for; matrix products, arithmetic and copies ran while one was open for 0% of the time, Pallas kernels for 35%

profile of v1, /device:TPU:0, one launch (start us, length us, event | category | flops | bytes accessed | tf_op | source)
XLA Modules:
  0.0 125.0 jit_solution(17686758257448766276)
XLA Ops:
  0.7 4.6 %prep.1 = (bf16[4,3,128,128]{3,2,1,0:T(8,128)(2,1)}, bf16[4,3,128,128]{3,2,1,0:T(8,128)(2,1)}, bf16[4,3,128,128]{3,2,1,0:T(8,128)(2,1)}, bf16[4,3,128,128]{3,2,1...) custom-call(bf16[128,4096]{1,0:T(8,128)(2,1)} %bitcast.12, ...), custom_call_target="tpu_custom_call" | custom-call | flops 10485760 | bytes 6291456 | tf_op jit(solution)/shard_map/prep/pallas_call | solution.py:85
  5.3 4.3 %prep_near.1 = bf16[4,4,3,128,128]{4,3,2,1,0:T(8,128)(2,1)} custom-call(bf16[128,4096]{1,0:T(8,128)(2,1)} %bitcast.6, bf16[128,4096]{1,0:T(8,128)(2,1)} %bitcast.8, bf16[128,4096]{1,0:T(8,128)(2,1)} %bitcast.10), custom_call_target="tpu_custom_call" | custom-call | flops 10485760 | bytes 4718592 | tf_op jit(solution)/shard_map/prep_near/pallas_call | solution.py:145
  9.6 0.4 collective-permute-start
  10.1 2.9 %collective-permute-start.5 = (bf16[4,3,128,128]{3,2,1,0:T(8,128)(2,1)}, bf16[4,3,128,128]{3,2,1,0:T(8,128)(2,1)S(1)}, u32[]{:S(2)}, u32[]{:S(2)}) collective-permute-start(bf16[4,3,128,128]{3,2,1,0:T(8,128)(2,1)} %get-tuple-element.55), channel_id=1, source_target_pairs={{0,2},{1,3},{2,0},{3,1},{4,6},{5,7},{6,4},{7,5},{8,10},{9,11},{10,... | collective-permute-start | bytes 1179656 | tf_op jit(solution)/shard_map/ppermute | solution.py:37
  13.0 1.5 %collective-permute-start.7 = (bf16[4,3,128,128]{3,2,1,0:T(8,128)(2,1)}, bf16[4,3,128,128]{3,2,1,0:T(8,128)(2,1)S(1)}, u32[]{:S(2)}, u32[]{:S(2)}) collective-permute-start(bf16[4,3,128,128]{3,2,1,0:T(8,128)(2,1)} %get-tuple-element.57), channel_id=1, source_target_pairs={{0,4},{1,5},{2,6},{3,7},{4,0},{5,1},{6,2},{7,3},{8,12},{9,13},{10,... | collective-permute-start | bytes 1179656 | tf_op jit(solution)/shard_map/ppermute | solution.py:37
  14.6 1.6 %collective-permute-start.8 = (bf16[4,3,128,128]{3,2,1,0:T(8,128)(2,1)}, bf16[4,3,128,128]{3,2,1,0:T(8,128)(2,1)S(1)}, u32[]{:S(2)}, u32[]{:S(2)}) collective-permute-start(bf16[4,3,128,128]{3,2,1,0:T(8,128)(2,1)} %get-tuple-element.58), channel_id=1, source_target_pairs={{0,5},{1,4},{2,7},{3,6},{4,1},{5,0},{6,3},{7,2},{8,13},{9,12},{10,... | collective-permute-start | bytes 1179656 | tf_op jit(solution)/shard_map/ppermute | solution.py:37
  16.1 7.0 %collective-permute-done.5.refs_2_.refs_7_ = bf16[4,3,128,128]{3,2,1,0:T(8,128)(2,1)S(1)} collective-permute-done((bf16[4,3,128,128]{3,2,1,0:T(8,128)(2,1)}, bf16[4,3,128,128]{3,2,1,0:T(8,128)(2,1)S(1)}, u32[]{:S(2)}, u32[]{:S(2)}) %collective-permute-start.5) | collective-permute-done | bytes 393248 | tf_op jit(solution)/shard_map/ppermute | solution.py:37
  23.1 3.0 %collective-permute-start.9 = (bf16[4,3,128,128]{3,2,1,0:T(8,128)(2,1)}, bf16[4,3,128,128]{3,2,1,0:T(8,128)(2,1)}, u32[]{:S(2)}, u32[]{:S(2)}) collective-permute-start(bf16[4,3,128,128]{3,2,1,0:T(8,128)(2,1)} %get-tuple-element.59), channel_id=1, source_target_pairs={{0,6},{1,7},{2,4},{3,5},{4,2},{5,3},{6,0},{7,1},{8,14},{9,15},{10,... | collective-permute-start | bytes 1179656 | tf_op jit(solution)/shard_map/ppermute | solution.py:37
  26.2 10.5 %all_to_all.15.refs_8_.refs_13_.gain_ref = f32[4,4,1024]{2,1,0:T(4,128)} all-to-all(f32[4,4,1024]{2,1,0:T(4,128)S(1)} %broadcast_in_dim.3), channel_id=1, replica_groups=mesh['fsdp'=4,'seq'=8] {'fsdp'}, dimensions={0} | all-to-all | bytes 131072 | tf_op jit(solution)/shard_map/all_to_all | solution.py:458
  36.7 5.1 %prep_pairs.1 = (bf16[2,3,3,128,128]{4,3,2,1,0:T(8,128)(2,1)}, bf16[2,3,3,128,128]{4,3,2,1,0:T(8,128)(2,1)}, bf16[2,3,3,128,128]{4,3,2,1,0:T(8,128)(2,1)}, bf16[...) custom-call(bf16[128,4096]{1,0:T(8,128)(2,1)} %bitcast.7, ...), custom_call_target="tpu_custom_call" | custom-call | flops 10485760 | bytes 7864320 | tf_op jit(solution)/shard_map/prep_pairs/pallas_call | solution.py:160
  41.8 0.7 copy-done.10
  42.5 0.5 collective-permute-start.1
  43.1 0.7 copy-done.11
  43.8 0.6 collective-permute-start.2
  44.5 5.2 %collective-permute-done.8.refs_5_.refs_10_ = bf16[4,3,128,128]{3,2,1,0:T(8,128)(2,1)S(1)} collective-permute-done((bf16[4,3,128,128]{3,2,1,0:T(8,128)(2,1)}, bf16[4,3,128,128]{3,2,1,0:T(8,128)(2,1)S(1)}, u32[]{:S(2)}, u32[]{:S(2)}) %collective-permute-start.8) | collective-permute-done | bytes 393248 | tf_op jit(solution)/shard_map/ppermute | solution.py:37
  49.7 0.7 copy-done.12
  50.4 2.7 %collective-permute-start.3 = (bf16[2,3,3,128,128]{4,3,2,1,0:T(8,128)(2,1)}, bf16[2,3,3,128,128]{4,3,2,1,0:T(8,128)(2,1)S(1)}, u32[]{:S(2)}, u32[]{:S(2)}) collective-permute-start(bf16[2,3,3,128,128]{4,3,2,1,0:T(8,128)(2,1)} %get-tuple-element.70), channel_id=1, source_target_pairs={{0,6},{1,7},{2,4},{3,5},{4,2},{5,3},{6,0},{7,1},{8,14},{9,15},{10,... | collective-permute-start | bytes 1769480 | tf_op jit(solution)/shard_map/ppermute | solution.py:37
  53.8 0.5 collective-permute-start.11
  54.3 0.3 collective-permute-start.12
  54.6 10.1 %student.1 = (bf16[8,4,128,128]{3,2,1,0:T(8,128)(2,1)}, f32[4,1024,128]{2,1,0:T(8,128)}) custom-call(bf16[4,3,128,128]{3,2,1,0:T(8,128)(2,1)} %get-tuple-element.75.refs_0_.refs_5_, bf16[4,3,128,128]{3,2,1,0:T(8,128)(2,1)} %copy-done.8, bf16[4,3,128,128]{3,2,1,0:T(8,128)(2,1)} %copy-done.9, bf16[4,3,128,128]{3,2,1,0:T(8,128)(2,1)} %copy-done.10, ...), custom_call_target="tpu_custom_call" | custom-call | flops 4294967296 | bytes 4194304 | tf_op jit(solution)/shard_map/student/pallas_call | solution.py:241
  64.7 2.8 %collective-permute-start.13 = (bf16[2,1,3,128,128]{4,3,2,1,0:T(8,128)(2,1)S(1)}, bf16[2,1,3,128,128]{4,3,2,1,0:T(8,128)(2,1)}, u32[]{:S(2)}, u32[]{:S(2)}) collective-permute-start(bf16[2,1,3,128,128]{4,3,2,1,0:T(8,128)(2,1)S(1)} %copy-done.14), channel_id=1, source_target_pairs={{0,6},{1,7},{2,4},{3,5},{4,2},{5,3},{6,0},{7,1},{8,14},{9,15},{10,... | collective-permute-start | bytes 589832 | tf_op jit(solution)/shard_map/ppermute | solution.py:37
  67.5 8.2 %collective-permute-done.2.refs_3_ = bf16[2,3,3,128,128]{4,3,2,1,0:T(8,128)(2,1)S(1)} collective-permute-done((bf16[2,3,3,128,128]{4,3,2,1,0:T(8,128)(2,1)}, bf16[2,3,3,128,128]{4,3,2,1,0:T(8,128)(2,1)S(1)}, u32[]{:S(2)}, u32[]{:S(2)}) %collective-permute-start.2) | collective-permute-done | bytes 589856 | tf_op jit(solution)/shard_map/ppermute | solution.py:37
  75.7 3.7 %all-to-all-start.1 = ((bf16[8,4,128,128]{3,2,1,0:T(8,128)(2,1)}), bf16[8,4,128,128]{3,2,1,0:T(8,128)(2,1)S(1)}, u32[]{:S(2)}, u32[]{:S(2)}) async-start(bf16[8,4,128,128]{3,2,1,0:T(8,128)(2,1)} %get-tuple-element.85.refs_14_), calls=%async_computation.1 | async-start | bytes 2097152 | tf_op jit(solution)/shard_map/all_to_all | solution.py:428
  79.5 17.6 %teacher.2.refs_16_ = f32[1,4,512]{2,1,0:T(4,128)} custom-call(s32[1]{0:T(128)S(6)} %copy.14.refs_0_, bf16[2,3,3,128,128]{4,3,2,1,0:T(8,128)(2,1)} %get-tuple-element.91.refs_1_, bf16[2,3,3,128,128]{4,3,2,1,0:T(8,128)(2,1)} %copy-done.5, bf16[2,3,3,128,128]{4,3,2,1,0:T(8,128)(2,1)} %copy-done.6, bf16[2,3,3,128,128]{4,3,2,1,0:T(8,128)(2,1)} %copy-done.7, ...), custom_call_target="tpu_custom_call" | custom-call | flops 9663676416 | bytes 6291456 | tf_op jit(solution)/shard_map/teacher/pallas_call | solution.py:328
  97.2 0.6 copy-done.15
  97.8 0.1 copy-done.16
  97.9 7.6 %teacher.3 = f32[32,4,512]{2,1,0:T(4,128)} custom-call(s32[1]{0:T(128)S(6)} %copy.14.refs_0_, bf16[2,1,3,128,128]{4,3,2,1,0:T(8,128)(2,1)} %get-tuple-element.86.refs_1_, bf16[2,1,3,128,128]{4,3,2,1,0:T(8,128)(2,1)} %copy-done.15, bf16[2,1,3,128,128]{4,3,2,1,0:T(8,128)(2,1)} %copy-done.16, bf16[2,1,3,128,128]{4,3,2,1,0:T(8,128)(2,1)} %collective-permute-done.13.refs_4_, ...), custom_call_target="tpu_custom_call" | custom-call | flops 3221225472 | bytes 2097152 | tf_op jit(solution)/shard_map/teacher/pallas_call | solution.py:328
  105.5 6.3 %all-to-all-start.2 = ((f32[32,4,512]{2,1,0:T(4,128)}), f32[32,4,512]{2,1,0:T(4,128)S(1)}, u32[]{:S(2)}, u32[]{:S(2)}) async-start(f32[32,4,512]{2,1,0:T(4,128)} %teacher.3), calls=%async_computation.2 | async-start | bytes 524288 | tf_op jit(solution)/shard_map/all_to_all | solution.py:488
  111.8 3.4 %assemble.1 = bf16[1,128,4096]{2,1,0:T(8,128)(2,1)} custom-call(bf16[8,4,128,128]{3,2,1,0:T(8,128)(2,1)} %copy-done), custom_call_target="tpu_custom_call" | custom-call | tf_op jit(solution)/shard_map/assemble/pallas_call | solution.py:404
  115.2 7.2 %all-to-all-done.2.terms_ref = f32[32,4,512]{2,1,0:T(4,128)S(1)} async-done(((f32[32,4,512]{2,1,0:T(4,128)}), f32[32,4,512]{2,1,0:T(4,128)S(1)}, u32[]{:S(2)}, u32[]{:S(2)}) %all-to-all-start.2) | async-done | bytes 262176 | tf_op jit(solution)/shard_map/all_to_all | solution.py:488
  122.4 0.7 copy-done.2
  123.1 1.8 %finish.1 = (f32[1]{0:T(128)}, f32[2,1024]{1,0:T(2,128)}, f32[2,1024]{1,0:T(2,128)}, f32[2,4096]{1,0:T(2,128)}) custom-call(f32[32,4,512]{2,1,0:T(4,128)} %copy-done.2, f32[4,4,1024]{2,1,0:T(4,128)} %all_to_all.15.refs_8_.refs_13_.gain_ref), custom_call_target="tpu_custom_call" | custom-call | tf_op jit(solution)/shard_map/finish/pallas_call | solution.py:380
  (45 shorter events, 0.2 us)
Async XLA Ops:
  0.6 4.6 %copy-start.3 = (f32[2,1024]{1,0:T(2,128)S(1)}, f32[2,1024]{1,0:T(2,128)}, u32[]{:S(2)}) copy-start(f32[2,1024]{1,0:T(2,128)} %param.17) | copy-start | bytes 24580
  0.6 4.6 %copy-start.4 = (f32[2,1024]{1,0:T(2,128)S(1)}, f32[2,1024]{1,0:T(2,128)}, u32[]{:S(2)}) copy-start(f32[2,1024]{1,0:T(2,128)} %param.16) | copy-start | bytes 24580
  5.2 4.8 %copy-start.13 = (bf16[4,3,128,128]{3,2,1,0:T(8,128)(2,1)S(1)}, bf16[4,3,128,128]{3,2,1,0:T(8,128)(2,1)}, u32[]{:S(2)}) copy-start(bf16[4,3,128,128]{3,2,1,0:T(8,128)(2,1)} %get-tuple-element.54) | copy-start | bytes 1179652
  9.6 16.6 %collective-permute-start = (bf16[4,4,3,128,128]{4,3,2,1,0:T(8,128)(2,1)}, bf16[4,4,3,128,128]{4,3,2,1,0:T(8,128)(2,1)S(1)}, u32[]{:S(2)}, u32[]{:S(2)}) collective-permute-start(bf16[4,4,3,128,128]{4,3,2,1,0:T(8,128)(2,1)} %prep_near.1), channel_id=1, source_target_pairs={{0,1},{1,0},{2,3},{3,2},{4,5},{5,4},{6,7},{7,6},{8,9},{9,8},{10,11... | collective-permute-start | bytes 4718600 | tf_op jit(solution)/shard_map/ppermute | solution.py:37
  10.0 4.5 %collective-permute-start.4 = (bf16[4,3,128,128]{3,2,1,0:T(8,128)(2,1)S(1)}, bf16[4,3,128,128]{3,2,1,0:T(8,128)(2,1)S(1)}, u32[]{:S(2)}, u32[]{:S(2)}) collective-permute-start(bf16[4,3,128,128]{3,2,1,0:T(8,128)(2,1)S(1)} %copy-done.13), channel_id=1, source_target_pairs={{0,1},{1,0},{2,3},{3,2},{4,5},{5,4},{6,7},{7,6},{8,9},{9,8},{10,11... | collective-permute-start | bytes 1179656 | tf_op jit(solution)/shard_map/ppermute | solution.py:37
  10.1 13.0 %collective-permute-start.5 = (bf16[4,3,128,128]{3,2,1,0:T(8,128)(2,1)}, bf16[4,3,128,128]{3,2,1,0:T(8,128)(2,1)S(1)}, u32[]{:S(2)}, u32[]{:S(2)}) collective-permute-start(bf16[4,3,128,128]{3,2,1,0:T(8,128)(2,1)} %get-tuple-element.55), channel_id=1, source_target_pairs={{0,2},{1,3},{2,0},{3,1},{4,6},{5,7},{6,4},{7,5},{8,10},{9,11},{10,... | collective-permute-start | bytes 1179656 | tf_op jit(solution)/shard_map/ppermute | solution.py:37
  13.0 28.7 %collective-permute-start.6 = (bf16[4,3,128,128]{3,2,1,0:T(8,128)(2,1)}, bf16[4,3,128,128]{3,2,1,0:T(8,128)(2,1)S(1)}, u32[]{:S(2)}, u32[]{:S(2)}) collective-permute-start(bf16[4,3,128,128]{3,2,1,0:T(8,128)(2,1)} %get-tuple-element.56), channel_id=1, source_target_pairs={{0,3},{1,2},{2,1},{3,0},{4,7},{5,6},{6,5},{7,4},{8,11},{9,10},{10,... | collective-permute-start | bytes 1179656 | tf_op jit(solution)/shard_map/ppermute | solution.py:37
  13.0 30.1 %collective-permute-start.7 = (bf16[4,3,128,128]{3,2,1,0:T(8,128)(2,1)}, bf16[4,3,128,128]{3,2,1,0:T(8,128)(2,1)S(1)}, u32[]{:S(2)}, u32[]{:S(2)}) collective-permute-start(bf16[4,3,128,128]{3,2,1,0:T(8,128)(2,1)} %get-tuple-element.57), channel_id=1, source_target_pairs={{0,4},{1,5},{2,6},{3,7},{4,0},{5,1},{6,2},{7,3},{8,12},{9,13},{10,... | collective-permute-start | bytes 1179656 | tf_op jit(solution)/shard_map/ppermute | solution.py:37
  14.6 40.1 %copy-start.8 = (bf16[4,3,128,128]{3,2,1,0:T(8,128)(2,1)}, bf16[4,3,128,128]{3,2,1,0:T(8,128)(2,1)S(1)}, u32[]{:S(2)}) copy-start(bf16[4,3,128,128]{3,2,1,0:T(8,128)(2,1)S(1)} %collective-permute-done.4.refs_1_.refs_6_) | copy-start | bytes 1179652
  14.6 35.1 %collective-permute-start.8 = (bf16[4,3,128,128]{3,2,1,0:T(8,128)(2,1)}, bf16[4,3,128,128]{3,2,1,0:T(8,128)(2,1)S(1)}, u32[]{:S(2)}, u32[]{:S(2)}) collective-permute-start(bf16[4,3,128,128]{3,2,1,0:T(8,128)(2,1)} %get-tuple-element.58), channel_id=1, source_target_pairs={{0,5},{1,4},{2,7},{3,6},{4,1},{5,0},{6,3},{7,2},{8,13},{9,12},{10,... | collective-permute-start | bytes 1179656 | tf_op jit(solution)/shard_map/ppermute | solution.py:37
  23.1 18.6 %copy-start.9 = (bf16[4,3,128,128]{3,2,1,0:T(8,128)(2,1)}, bf16[4,3,128,128]{3,2,1,0:T(8,128)(2,1)S(1)}, u32[]{:S(2)}) copy-start(bf16[4,3,128,128]{3,2,1,0:T(8,128)(2,1)S(1)} %collective-permute-done.5.refs_2_.refs_7_) | copy-start | bytes 1179652
  23.1 30.6 %collective-permute-start.9 = (bf16[4,3,128,128]{3,2,1,0:T(8,128)(2,1)}, bf16[4,3,128,128]{3,2,1,0:T(8,128)(2,1)}, u32[]{:S(2)}, u32[]{:S(2)}) collective-permute-start(bf16[4,3,128,128]{3,2,1,0:T(8,128)(2,1)} %get-tuple-element.59), channel_id=1, source_target_pairs={{0,6},{1,7},{2,4},{3,5},{4,2},{5,3},{6,0},{7,1},{8,14},{9,15},{10,... | collective-permute-start | bytes 1179656 | tf_op jit(solution)/shard_map/ppermute | solution.py:37
  26.2 10.6 %copy-start.1 = (bf16[4,4,3,128,128]{4,3,2,1,0:T(8,128)(2,1)}, bf16[4,4,3,128,128]{4,3,2,1,0:T(8,128)(2,1)S(1)}, u32[]{:S(2)}) copy-start(bf16[4,4,3,128,128]{4,3,2,1,0:T(8,128)(2,1)S(1)} %collective-permute-done.refs_3_) | copy-start | bytes 4718596
  26.2 27.6 %collective-permute-start.10 = (bf16[4,3,128,128]{3,2,1,0:T(8,128)(2,1)}, bf16[4,3,128,128]{3,2,1,0:T(8,128)(2,1)}, u32[]{:S(2)}, u32[]{:S(2)}) collective-permute-start(bf16[4,3,128,128]{3,2,1,0:T(8,128)(2,1)} %get-tuple-element.60), channel_id=1, source_target_pairs={{0,7},{1,6},{2,5},{3,4},{4,3},{5,2},{6,1},{7,0},{8,15},{9,14},{10,... | collective-permute-start | bytes 1179656 | tf_op jit(solution)/shard_map/ppermute | solution.py:37
  41.8 0.8 copy-start.10
  42.5 22.1 %collective-permute-start.1 = (bf16[2,3,3,128,128]{4,3,2,1,0:T(8,128)(2,1)}, bf16[2,3,3,128,128]{4,3,2,1,0:T(8,128)(2,1)S(1)}, u32[]{:S(2)}, u32[]{:S(2)}) collective-permute-start(bf16[2,3,3,128,128]{4,3,2,1,0:T(8,128)(2,1)} %get-tuple-element.68), channel_id=1, source_target_pairs={{0,2},{1,3},{2,0},{3,1},{4,6},{5,7},{6,4},{7,5},{8,10},{9,11},{10,... | collective-permute-start | bytes 1769480 | tf_op jit(solution)/shard_map/ppermute | solution.py:37
  43.1 0.8 copy-start.11
  43.8 31.9 %collective-permute-start.2 = (bf16[2,3,3,128,128]{4,3,2,1,0:T(8,128)(2,1)}, bf16[2,3,3,128,128]{4,3,2,1,0:T(8,128)(2,1)S(1)}, u32[]{:S(2)}, u32[]{:S(2)}) collective-permute-start(bf16[2,3,3,128,128]{4,3,2,1,0:T(8,128)(2,1)} %get-tuple-element.69), channel_id=1, source_target_pairs={{0,4},{1,5},{2,6},{3,7},{4,0},{5,1},{6,2},{7,3},{8,12},{9,13},{10,... | collective-permute-start | bytes 1769480 | tf_op jit(solution)/shard_map/ppermute | solution.py:37
  49.7 0.7 copy-start.12
  50.4 25.3 %collective-permute-start.3 = (bf16[2,3,3,128,128]{4,3,2,1,0:T(8,128)(2,1)}, bf16[2,3,3,128,128]{4,3,2,1,0:T(8,128)(2,1)S(1)}, u32[]{:S(2)}, u32[]{:S(2)}) collective-permute-start(bf16[2,3,3,128,128]{4,3,2,1,0:T(8,128)(2,1)} %get-tuple-element.70), channel_id=1, source_target_pairs={{0,6},{1,7},{2,4},{3,5},{4,2},{5,3},{6,0},{7,1},{8,14},{9,15},{10,... | collective-permute-start | bytes 1769480 | tf_op jit(solution)/shard_map/ppermute | solution.py:37
  53.8 10.9 %copy-start.14 = (bf16[2,1,3,128,128]{4,3,2,1,0:T(8,128)(2,1)S(1)}, bf16[2,1,3,128,128]{4,3,2,1,0:T(8,128)(2,1)}, u32[]{:S(2)}) copy-start(bf16[2,1,3,128,128]{4,3,2,1,0:T(8,128)(2,1)} %get-tuple-element.89) | copy-start | bytes 589828
  53.8 43.3 %collective-permute-start.11 = (bf16[2,1,3,128,128]{4,3,2,1,0:T(8,128)(2,1)}, bf16[2,1,3,128,128]{4,3,2,1,0:T(8,128)(2,1)S(1)}, u32[]{:S(2)}, u32[]{:S(2)}) collective-permute-start(bf16[2,1,3,128,128]{4,3,2,1,0:T(8,128)(2,1)} %get-tuple-element.87), channel_id=1, source_target_pairs={{0,2},{1,3},{2,0},{3,1},{4,6},{5,7},{6,4},{7,5},{8,10},{9,11},{10,... | collective-permute-start | bytes 589832 | tf_op jit(solution)/shard_map/ppermute | solution.py:37
  54.3 42.8 %collective-permute-start.12 = (bf16[2,1,3,128,128]{4,3,2,1,0:T(8,128)(2,1)}, bf16[2,1,3,128,128]{4,3,2,1,0:T(8,128)(2,1)S(1)}, u32[]{:S(2)}, u32[]{:S(2)}) collective-permute-start(bf16[2,1,3,128,128]{4,3,2,1,0:T(8,128)(2,1)} %get-tuple-element.88), channel_id=1, source_target_pairs={{0,4},{1,5},{2,6},{3,7},{4,0},{5,1},{6,2},{7,3},{8,12},{9,13},{10,... | collective-permute-start | bytes 589832 | tf_op jit(solution)/shard_map/ppermute | solution.py:37
  64.7 14.8 %copy-start.5 = (bf16[2,3,3,128,128]{4,3,2,1,0:T(8,128)(2,1)}, bf16[2,3,3,128,128]{4,3,2,1,0:T(8,128)(2,1)S(1)}, u32[]{:S(2)}) copy-start(bf16[2,3,3,128,128]{4,3,2,1,0:T(8,128)(2,1)S(1)} %collective-permute-done.1.refs_2_) | copy-start | bytes 1769476
  64.7 32.5 %collective-permute-start.13 = (bf16[2,1,3,128,128]{4,3,2,1,0:T(8,128)(2,1)S(1)}, bf16[2,1,3,128,128]{4,3,2,1,0:T(8,128)(2,1)}, u32[]{:S(2)}, u32[]{:S(2)}) collective-permute-start(bf16[2,1,3,128,128]{4,3,2,1,0:T(8,128)(2,1)S(1)} %copy-done.14), channel_id=1, source_target_pairs={{0,6},{1,7},{2,4},{3,5},{4,2},{5,3},{6,0},{7,1},{8,14},{9,15},{10,... | collective-permute-start | bytes 589832 | tf_op jit(solution)/shard_map/ppermute | solution.py:37
  75.7 3.8 %copy-start.6 = (bf16[2,3,3,128,128]{4,3,2,1,0:T(8,128)(2,1)}, bf16[2,3,3,128,128]{4,3,2,1,0:T(8,128)(2,1)S(1)}, u32[]{:S(2)}) copy-start(bf16[2,3,3,128,128]{4,3,2,1,0:T(8,128)(2,1)S(1)} %collective-permute-done.2.refs_3_) | copy-start | bytes 1769476
  75.7 3.8 %copy-start.7 = (bf16[2,3,3,128,128]{4,3,2,1,0:T(8,128)(2,1)}, bf16[2,3,3,128,128]{4,3,2,1,0:T(8,128)(2,1)S(1)}, u32[]{:S(2)}) copy-start(bf16[2,3,3,128,128]{4,3,2,1,0:T(8,128)(2,1)S(1)} %collective-permute-done.3.refs_4_) | copy-start | bytes 1769476
  75.7 29.8 %all-to-all-start.1 = ((bf16[8,4,128,128]{3,2,1,0:T(8,128)(2,1)}), bf16[8,4,128,128]{3,2,1,0:T(8,128)(2,1)S(1)}, u32[]{:S(2)}, u32[]{:S(2)}) async-start(bf16[8,4,128,128]{3,2,1,0:T(8,128)(2,1)} %get-tuple-element.85.refs_14_), calls=%async_computation.1 | async-start | bytes 2097152 | tf_op jit(solution)/shard_map/all_to_all | solution.py:428
  97.2 0.8 copy-start.16
  105.5 6.3 %copy-start = (bf16[8,4,128,128]{3,2,1,0:T(8,128)(2,1)}, bf16[8,4,128,128]{3,2,1,0:T(8,128)(2,1)S(1)}, u32[]{:S(2)}) copy-start(bf16[8,4,128,128]{3,2,1,0:T(8,128)(2,1)S(1)} %all-to-all-done.1.parts_ref) | copy-start | bytes 3145732
  105.5 16.9 %all-to-all-start.2 = ((f32[32,4,512]{2,1,0:T(4,128)}), f32[32,4,512]{2,1,0:T(4,128)S(1)}, u32[]{:S(2)}, u32[]{:S(2)}) async-start(f32[32,4,512]{2,1,0:T(4,128)} %teacher.3), calls=%async_computation.2 | async-start | bytes 524288 | tf_op jit(solution)/shard_map/all_to_all | solution.py:488
  122.4 0.7 copy-start.2
  (1 other events, 0.7 us)

commit v2 on v1

--- a/solution.py
+++ b/solution.py
@@ -71,7 +71,7 @@
 
 def prep(q, k, v, groups, width, plans):
     tokens, inner = q.shape
-    rows = min(32, tokens)
+    rows = min(64, tokens)
     shapes, specs = [], []
     for _, columns, by_step in plans:
         heads = columns // HEAD_DIM
@@ -137,7 +137,7 @@
 def prep_pairs(q, k, v, groups, width, counts, near):
     tokens, inner = q.shape
     heads = width // HEAD_DIM
-    rows = min(32, tokens)
+    rows = min(64, tokens)
     in_specs = [pl.BlockSpec((rows, inner), lambda i: (i, 0))] * 3
     near_spec = pl.BlockSpec((groups // 2, heads, 3, rows, HEAD_DIM), lambda i: (0, 0, 0, i, 0))
     near_shape = jax.ShapeDtypeStruct((groups // 2, heads, 3, tokens, HEAD_DIM), bf16)
@@ -286,17 +286,20 @@
     squares = jnp.zeros((1, HEAD_DIM), f32)
     term_q = jnp.zeros((1, HEAD_DIM), f32)
     key_grad = None
+    scores = nt(qt[0:block, :], kt[...])
+    student_scores = nt(qs[0:block, :], ks[...])
     for start in range(0, length, block):
         rows = pl.ds(start, block)
         slots = range(start // tokens, start // tokens + block // tokens)
-        scores = nt(qt[rows, :], kt[...])
-        student_scores = nt(qs[rows, :], ks[...])
         probs, _ = probabilities(scores)
         target = nn(probs.astype(bf16), vt[...]).astype(bf16)
         out = jnp.concatenate([out_ref[me ^ slot, 0] for slot in slots], axis=0)
         diff = out.astype(f32) - target.astype(f32)
         squares = squares + jnp.sum(diff * diff, axis=0, keepdims=True)
         error = (2.0 * share * diff).astype(bf16)
+        later = start + block
+        if later < length:
+            following = nt(qt[later : later + block, :], kt[...]), nt(qs[later : later + block, :], ks[...])
         dprob = nt(error, vs[...])
         lse = jnp.concatenate([lse_ref[0, rows, :]] * (length // HEAD_DIM), axis=1)
         probs = jnp.exp2(student_scores * factor - lse)
@@ -307,6 +310,8 @@
         term_q = term_q + jnp.sum(dquery.astype(f32) * unit.astype(f32), axis=0, keepdims=True)
         part = nn(jnp.transpose(qs[rows, :]), dscore)
         key_grad = part if key_grad is None else key_grad + part
+        if later < length:
+            scores, student_scores = following
     dkey = (jnp.transpose(key_grad) * scale).astype(bf16)
     unit = jnp.concatenate([part_at(student_refs, me, slot, 1) for slot in range(groups)], axis=0)
     term_k = jnp.sum(dkey.astype(f32) * unit.astype(f32), axis=0, keepdims=True)
@@ -445,7 +450,7 @@
     inner = query_teacher.shape[2]
     width = inner // groups
     heads = width // HEAD_DIM
-    split = max(heads - 1, 1) * HEAD_DIM
+    split = (heads + 1) // 2 * HEAD_DIM
 
     sent = prep(query_student[0], key_student[0], value_student[0], groups, width, [(0, width, True)])
     student_parts = by_step(sent)
@@ -460,7 +465,8 @@
     sent = prep_pairs(*later, groups, width, counts, near)
     first_sent, second_sent = sent[: groups // 2], sent[groups // 2 :]
     teacher_first = by_pairs(first_sent)
-    student_parts, second_sent = lax.optimization_barrier((student_parts, second_sent))
+    ahead, second_sent = lax.optimization_barrier((teacher_first[1], second_sent))
+    teacher_first[1] = ahead
     teacher_second = by_pairs(second_sent)
     out, lse = student(student_parts, gains, groups, tokens, width)
     teacher_first, going = lax.optimization_barrier((teacher_first, out))

time: 126 us -> 117 us (0.929)
  blocking collectives: 10.5 us -> 0 us
  starting transfers between devices: 27.1 us -> 34.7 us
  Pallas kernels: 54.4 us -> 48.5 us
  waiting for transfers between devices: 27.6 us -> 29.1 us
    all_to_all x1 -> x0, blocking collectives: 10.5 us -> none  [local(): lax.all_to_all(own_gains, 'fsdp', split_axis=0, concat_axis=0, tiled=True)]
    all_to_all x0 -> x1, waiting for transfers between devices: none -> 5.09 us  [local(): lax.all_to_all(own_gains, 'fsdp', split_axis=0, concat_axis=0, tiled=True)]
    all_to_all x0 -> x1, starting transfers between devices: none -> 4.87 us  [local(): lax.all_to_all(own_gains, 'fsdp', split_axis=0, concat_axis=0, tiled=True)]
    ppermute x14, waiting for transfers between devices: 20.4 us -> 16.8 us  [swap(): return lax.ppermute(x, axis, [(i, i ^ step) for i in range(size)])]
    pallas_call x2, Pallas kernels: 25.2 us -> 22.5 us  [teacher(): pl.pallas_call(functools.partial(teacher_kernel, groups, tokens, width, f...]
    all_to_all x1, starting transfers between devices: 6.29 us -> 8.84 us  [local(): lax.all_to_all(grads, ('fsdp', 'seq'), split_axis=0, concat_axis=0, tiled...]
    unnamed x34 -> x38, local copies, waits for them, and re-layouts: 3.73 us -> 2.26 us
  transfers between devices with their start and end apart: 16 -> 17, of which waited for: 4 -> 6; matrix products, arithmetic and copies ran while one was open for 0% -> 1% of each run, Pallas kernels for 35% -> 34%
where the time goes in v2:
time: 117 us
  Pallas kernels  48.5 us (41%)
  starting transfers between devices  34.7 us (30%)
  waiting for transfers between devices  29.1 us (25%)
  local copies, waits for them, and re-layouts  2.96 us (3%)
  between operations  1.66 us (1%)
    pallas_call x2, Pallas kernels, teacher(): pl.pallas_call(functools.partial(teacher_kernel, groups, tokens, width, f...  22.5 us
    ppermute x14, starting transfers between devices, swap(): return lax.ppermute(x, axis, [(i, i ^ step) for i in range(size)])  17.3 us
    ppermute x14, waiting for transfers between devices, swap(): return lax.ppermute(x, axis, [(i, i ^ step) for i in range(size)])  16.8 us
    pallas_call x1, Pallas kernels, student(): pl.pallas_call(functools.partial(student_kernel, groups, tokens, width, l...  10.1 us
    all_to_all x1, starting transfers between devices, local(): lax.all_to_all(grads, ('fsdp', 'seq'), split_axis=0, concat_axis=0, tiled...  8.84 us
    all_to_all x1, waiting for transfers between devices, local(): lax.all_to_all(grads, ('fsdp', 'seq'), split_axis=0, concat_axis=0, tiled...  7.15 us
    all_to_all x1, waiting for transfers between devices, local(): lax.all_to_all(own_gains, 'fsdp', split_axis=0, concat_axis=0, tiled=True)  5.09 us
    all_to_all x1, starting transfers between devices, local(): lax.all_to_all(own_gains, 'fsdp', split_axis=0, concat_axis=0, tiled=True)  4.87 us
  transfers between devices with their start and end apart: 17, of which 6 were waited for; matrix products, arithmetic and copies ran while one was open for 1% of the time, Pallas kernels for 34%

profile of v2, /device:TPU:0, one launch (start us, length us, event | category | flops | bytes accessed | tf_op | source)
XLA Modules:
  0.0 116.9 jit_solution(17062270596115562806)
XLA Ops:
  0.7 3.5 %prep.1 = (bf16[4,3,128,128]{3,2,1,0:T(8,128)(2,1)}, bf16[4,3,128,128]{3,2,1,0:T(8,128)(2,1)}, bf16[4,3,128,128]{3,2,1,0:T(8,128)(2,1)}, bf16[4,3,128,128]{3,2,1...) custom-call(bf16[128,4096]{1,0:T(8,128)(2,1)} %bitcast.12, ...), custom_call_target="tpu_custom_call" | custom-call | flops 10485760 | bytes 6291456 | tf_op jit(solution)/shard_map/prep/pallas_call | solution.py:85
  4.2 3.2 %prep_near.1 = bf16[4,4,3,128,128]{4,3,2,1,0:T(8,128)(2,1)} custom-call(bf16[128,4096]{1,0:T(8,128)(2,1)} %bitcast.6, bf16[128,4096]{1,0:T(8,128)(2,1)} %bitcast.8, bf16[128,4096]{1,0:T(8,128)(2,1)} %bitcast.10), custom_call_target="tpu_custom_call" | custom-call | flops 10485760 | bytes 4718592 | tf_op jit(solution)/shard_map/prep_near/pallas_call | solution.py:145
  7.4 0.4 collective-permute-start
  8.0 2.9 %collective-permute-start.5 = (bf16[4,3,128,128]{3,2,1,0:T(8,128)(2,1)S(1)}, bf16[4,3,128,128]{3,2,1,0:T(8,128)(2,1)S(1)}, u32[]{:S(2)}, u32[]{:S(2)}) collective-permute-start(bf16[4,3,128,128]{3,2,1,0:T(8,128)(2,1)S(1)} %copy-done.17), channel_id=1, source_target_pairs={{0,2},{1,3},{2,0},{3,1},{4,6},{5,7},{6,4},{7,5},{8,10},{9,11},{10,... | collective-permute-start | bytes 1179656 | tf_op jit(solution)/shard_map/ppermute | solution.py:37
  10.9 1.5 %collective-permute-start.7 = (bf16[4,3,128,128]{3,2,1,0:T(8,128)(2,1)}, bf16[4,3,128,128]{3,2,1,0:T(8,128)(2,1)S(1)}, u32[]{:S(2)}, u32[]{:S(2)}) collective-permute-start(bf16[4,3,128,128]{3,2,1,0:T(8,128)(2,1)} %get-tuple-element.50), channel_id=1, source_target_pairs={{0,4},{1,5},{2,6},{3,7},{4,0},{5,1},{6,2},{7,3},{8,12},{9,13},{10,... | collective-permute-start | bytes 1179656 | tf_op jit(solution)/shard_map/ppermute | solution.py:37
  12.4 1.6 %collective-permute-start.8 = (bf16[4,3,128,128]{3,2,1,0:T(8,128)(2,1)}, bf16[4,3,128,128]{3,2,1,0:T(8,128)(2,1)}, u32[]{:S(2)}, u32[]{:S(2)}) collective-permute-start(bf16[4,3,128,128]{3,2,1,0:T(8,128)(2,1)} %get-tuple-element.51), channel_id=1, source_target_pairs={{0,5},{1,4},{2,7},{3,6},{4,1},{5,0},{6,3},{7,2},{8,13},{9,12},{10,... | collective-permute-start | bytes 1179656 | tf_op jit(solution)/shard_map/ppermute | solution.py:37
  14.0 6.8 %collective-permute-done.5.refs_2_.refs_7_ = bf16[4,3,128,128]{3,2,1,0:T(8,128)(2,1)S(1)} collective-permute-done((bf16[4,3,128,128]{3,2,1,0:T(8,128)(2,1)S(1)}, bf16[4,3,128,128]{3,2,1,0:T(8,128)(2,1)S(1)}, u32[]{:S(2)}, u32[]{:S(2)}) %collective-permute-start.5) | collective-permute-done | bytes 393248 | tf_op jit(solution)/shard_map/ppermute | solution.py:37
  20.8 3.0 %collective-permute-start.9 = (bf16[4,3,128,128]{3,2,1,0:T(8,128)(2,1)}, bf16[4,3,128,128]{3,2,1,0:T(8,128)(2,1)}, u32[]{:S(2)}, u32[]{:S(2)}) collective-permute-start(bf16[4,3,128,128]{3,2,1,0:T(8,128)(2,1)} %get-tuple-element.52), channel_id=1, source_target_pairs={{0,6},{1,7},{2,4},{3,5},{4,2},{5,3},{6,0},{7,1},{8,14},{9,15},{10,... | collective-permute-start | bytes 1179656 | tf_op jit(solution)/shard_map/ppermute | solution.py:37
  23.8 0.7 broadcast_in_dim.3
  24.5 4.9 %all-to-all-start = ((f32[4,4,1024]{2,1,0:T(4,128)}), f32[4,4,1024]{2,1,0:T(4,128)S(1)}, u32[]{:S(2)}, u32[]{:S(2)}) async-start(f32[4,4,1024]{2,1,0:T(4,128)} %broadcast_in_dim.3), calls=%async_computation | async-start | bytes 131072 | tf_op jit(solution)/shard_map/all_to_all | solution.py:463
  30.1 5.1 %all-to-all-done.refs_8_.refs_13_.gain_ref = f32[4,4,1024]{2,1,0:T(4,128)S(1)} async-done(((f32[4,4,1024]{2,1,0:T(4,128)}), f32[4,4,1024]{2,1,0:T(4,128)S(1)}, u32[]{:S(2)}, u32[]{:S(2)}) %all-to-all-start) | async-done | bytes 65568 | tf_op jit(solution)/shard_map/all_to_all | solution.py:463
  35.1 4.0 %prep_pairs.1 = (bf16[2,2,3,128,128]{4,3,2,1,0:T(8,128)(2,1)}, bf16[2,2,3,128,128]{4,3,2,1,0:T(8,128)(2,1)}, bf16[2,2,3,128,128]{4,3,2,1,0:T(8,128)(2,1)}, bf16[...) custom-call(bf16[128,4096]{1,0:T(8,128)(2,1)} %bitcast.7, ...), custom_call_target="tpu_custom_call" | custom-call | flops 10485760 | bytes 7864320 | tf_op jit(solution)/shard_map/prep_pairs/pallas_call | solution.py:160
  39.2 0.6 collective-permute-start.1
  39.8 0.7 collective-permute-start.2
  40.5 7.0 %collective-permute-done.8.refs_5_.refs_10_ = bf16[4,3,128,128]{3,2,1,0:T(8,128)(2,1)} collective-permute-done((bf16[4,3,128,128]{3,2,1,0:T(8,128)(2,1)}, bf16[4,3,128,128]{3,2,1,0:T(8,128)(2,1)}, u32[]{:S(2)}, u32[]{:S(2)}) %collective-permute-start.8) | collective-permute-done | bytes 393248 | tf_op jit(solution)/shard_map/ppermute | solution.py:37
  47.5 2.8 %collective-permute-start.3 = (bf16[2,2,3,128,128]{4,3,2,1,0:T(8,128)(2,1)}, bf16[2,2,3,128,128]{4,3,2,1,0:T(8,128)(2,1)S(1)}, u32[]{:S(2)}, u32[]{:S(2)}) collective-permute-start(bf16[2,2,3,128,128]{4,3,2,1,0:T(8,128)(2,1)} %get-tuple-element.68), channel_id=1, source_target_pairs={{0,6},{1,7},{2,4},{3,5},{4,2},{5,3},{6,0},{7,1},{8,14},{9,15},{10,... | collective-permute-start | bytes 1179656 | tf_op jit(solution)/shard_map/ppermute | solution.py:37
  50.4 10.1 %student.1 = (bf16[8,4,128,128]{3,2,1,0:T(8,128)(2,1)}, f32[4,1024,128]{2,1,0:T(8,128)}) custom-call(bf16[4,3,128,128]{3,2,1,0:T(8,128)(2,1)} %get-tuple-element.46.refs_0_.refs_5_, bf16[4,3,128,128]{3,2,1,0:T(8,128)(2,1)} %copy-done.6, bf16[4,3,128,128]{3,2,1,0:T(8,128)(2,1)} %copy-done.7, bf16[4,3,128,128]{3,2,1,0:T(8,128)(2,1)} %copy-done.8, ...), custom_call_target="tpu_custom_call" | custom-call | flops 4294967296 | bytes 4194304 | tf_op jit(solution)/shard_map/student/pallas_call | solution.py:241
  60.5 0.5 collective-permute-start.11
  61.0 0.2 collective-permute-start.12
  61.2 2.8 %collective-permute-start.13 = (bf16[2,2,3,128,128]{4,3,2,1,0:T(8,128)(2,1)S(1)}, bf16[2,2,3,128,128]{4,3,2,1,0:T(8,128)(2,1)S(1)}, u32[]{:S(2)}, u32[]{:S(2)}) collective-permute-start(bf16[2,2,3,128,128]{4,3,2,1,0:T(8,128)(2,1)S(1)} %copy-done.10), channel_id=1, source_target_pairs={{0,6},{1,7},{2,4},{3,5},{4,2},{5,3},{6,0},{7,1},{8,14},{9,15},{10,... | collective-permute-start | bytes 1179656 | tf_op jit(solution)/shard_map/ppermute | solution.py:37
  64.0 1.1 collective-permute-done.2.refs_3_
  65.2 3.7 %all-to-all-start.1 = ((bf16[8,4,128,128]{3,2,1,0:T(8,128)(2,1)}), bf16[8,4,128,128]{3,2,1,0:T(8,128)(2,1)S(1)}, u32[]{:S(2)}, u32[]{:S(2)}) async-start(bf16[8,4,128,128]{3,2,1,0:T(8,128)(2,1)} %get-tuple-element.71.refs_14_), calls=%async_computation.1 | async-start | bytes 2097152 | tf_op jit(solution)/shard_map/all_to_all | solution.py:433
  68.9 11.2 %teacher.2.refs_16_ = f32[1,4,512]{2,1,0:T(4,128)} custom-call(s32[1]{0:T(128)S(6)} %copy.14.refs_0_, bf16[2,2,3,128,128]{4,3,2,1,0:T(8,128)(2,1)} %get-tuple-element.77.refs_1_, bf16[2,2,3,128,128]{4,3,2,1,0:T(8,128)(2,1)} %copy-done.11, bf16[2,2,3,128,128]{4,3,2,1,0:T(8,128)(2,1)} %copy-done.12, bf16[2,2,3,128,128]{4,3,2,1,0:T(8,128)(2,1)} %copy-done.15, ...), custom_call_target="tpu_custom_call" | custom-call | flops 6442450944 | bytes 4194304 | tf_op jit(solution)/shard_map/teacher/pallas_call | solution.py:333
  80.2 1.9 %collective-permute-done.12.refs_3_ = bf16[2,2,3,128,128]{4,3,2,1,0:T(8,128)(2,1)S(1)} collective-permute-done((bf16[2,2,3,128,128]{4,3,2,1,0:T(8,128)(2,1)}, bf16[2,2,3,128,128]{4,3,2,1,0:T(8,128)(2,1)S(1)}, u32[]{:S(2)}, u32[]{:S(2)}) %collective-permute-start.12) | collective-permute-done | bytes 393248 | tf_op jit(solution)/shard_map/ppermute | solution.py:37
  82.0 0.7 copy-done.14
  82.8 0.8 copy-done.16
  83.5 11.3 %teacher.3 = f32[32,4,512]{2,1,0:T(4,128)} custom-call(s32[1]{0:T(128)S(6)} %copy.14.refs_0_, bf16[2,2,3,128,128]{4,3,2,1,0:T(8,128)(2,1)} %get-tuple-element.72.refs_1_, bf16[2,2,3,128,128]{4,3,2,1,0:T(8,128)(2,1)} %copy-done.13, bf16[2,2,3,128,128]{4,3,2,1,0:T(8,128)(2,1)} %copy-done.14, bf16[2,2,3,128,128]{4,3,2,1,0:T(8,128)(2,1)} %copy-done.16, ...), custom_call_target="tpu_custom_call" | custom-call | flops 6442450944 | bytes 4194304 | tf_op jit(solution)/shard_map/teacher/pallas_call | solution.py:333
  94.9 8.8 %all-to-all-start.2 = ((f32[32,4,512]{2,1,0:T(4,128)}), f32[32,4,512]{2,1,0:T(4,128)S(1)}, u32[]{:S(2)}, u32[]{:S(2)}) async-start(f32[32,4,512]{2,1,0:T(4,128)} %teacher.3), calls=%async_computation.2 | async-start | bytes 524288 | tf_op jit(solution)/shard_map/all_to_all | solution.py:494
  103.7 3.4 %assemble.1 = bf16[1,128,4096]{2,1,0:T(8,128)(2,1)} custom-call(bf16[8,4,128,128]{3,2,1,0:T(8,128)(2,1)} %copy-done), custom_call_target="tpu_custom_call" | custom-call | tf_op jit(solution)/shard_map/assemble/pallas_call | solution.py:409
  107.2 7.2 %all-to-all-done.2.terms_ref = f32[32,4,512]{2,1,0:T(4,128)S(1)} async-done(((f32[32,4,512]{2,1,0:T(4,128)}), f32[32,4,512]{2,1,0:T(4,128)S(1)}, u32[]{:S(2)}, u32[]{:S(2)}) %all-to-all-start.2) | async-done | bytes 262176 | tf_op jit(solution)/shard_map/all_to_all | solution.py:494
  114.3 0.7 copy-done.2
  115.0 1.8 %finish.1 = (f32[1]{0:T(128)}, f32[2,1024]{1,0:T(2,128)}, f32[2,1024]{1,0:T(2,128)}, f32[2,4096]{1,0:T(2,128)}) custom-call(f32[32,4,512]{2,1,0:T(4,128)} %copy-done.2, f32[4,4,1024]{2,1,0:T(4,128)} %copy-done.3), custom_call_target="tpu_custom_call" | custom-call | tf_op jit(solution)/shard_map/finish/pallas_call | solution.py:385
  (50 shorter events, 0.2 us)
Async XLA Ops:
  0.6 3.5 %copy-start.4 = (f32[2,1024]{1,0:T(2,128)S(1)}, f32[2,1024]{1,0:T(2,128)}, u32[]{:S(2)}) copy-start(f32[2,1024]{1,0:T(2,128)} %param.17) | copy-start | bytes 24580
  0.6 3.5 %copy-start.5 = (f32[2,1024]{1,0:T(2,128)S(1)}, f32[2,1024]{1,0:T(2,128)}, u32[]{:S(2)}) copy-start(f32[2,1024]{1,0:T(2,128)} %param.16) | copy-start | bytes 24580
  4.2 3.7 %copy-start.18 = (bf16[4,3,128,128]{3,2,1,0:T(8,128)(2,1)S(1)}, bf16[4,3,128,128]{3,2,1,0:T(8,128)(2,1)}, u32[]{:S(2)}) copy-start(bf16[4,3,128,128]{3,2,1,0:T(8,128)(2,1)} %get-tuple-element.47) | copy-start | bytes 1179652
  4.2 3.8 %copy-start.17 = (bf16[4,3,128,128]{3,2,1,0:T(8,128)(2,1)S(1)}, bf16[4,3,128,128]{3,2,1,0:T(8,128)(2,1)}, u32[]{:S(2)}) copy-start(bf16[4,3,128,128]{3,2,1,0:T(8,128)(2,1)} %get-tuple-element.48) | copy-start | bytes 1179652
  7.4 16.4 %collective-permute-start = (bf16[4,4,3,128,128]{4,3,2,1,0:T(8,128)(2,1)}, bf16[4,4,3,128,128]{4,3,2,1,0:T(8,128)(2,1)S(1)}, u32[]{:S(2)}, u32[]{:S(2)}) collective-permute-start(bf16[4,4,3,128,128]{4,3,2,1,0:T(8,128)(2,1)} %prep_near.1), channel_id=1, source_target_pairs={{0,1},{1,0},{2,3},{3,2},{4,5},{5,4},{6,7},{7,6},{8,9},{9,8},{10,11... | collective-permute-start | bytes 4718600 | tf_op jit(solution)/shard_map/ppermute | solution.py:37
  7.9 4.5 %collective-permute-start.4 = (bf16[4,3,128,128]{3,2,1,0:T(8,128)(2,1)S(1)}, bf16[4,3,128,128]{3,2,1,0:T(8,128)(2,1)S(1)}, u32[]{:S(2)}, u32[]{:S(2)}) collective-permute-start(bf16[4,3,128,128]{3,2,1,0:T(8,128)(2,1)S(1)} %copy-done.18), channel_id=1, source_target_pairs={{0,1},{1,0},{2,3},{3,2},{4,5},{5,4},{6,7},{7,6},{8,9},{9,8},{10,11... | collective-permute-start | bytes 1179656 | tf_op jit(solution)/shard_map/ppermute | solution.py:37
  8.0 12.8 %collective-permute-start.5 = (bf16[4,3,128,128]{3,2,1,0:T(8,128)(2,1)S(1)}, bf16[4,3,128,128]{3,2,1,0:T(8,128)(2,1)S(1)}, u32[]{:S(2)}, u32[]{:S(2)}) collective-permute-start(bf16[4,3,128,128]{3,2,1,0:T(8,128)(2,1)S(1)} %copy-done.17), channel_id=1, source_target_pairs={{0,2},{1,3},{2,0},{3,1},{4,6},{5,7},{6,4},{7,5},{8,10},{9,11},{10,... | collective-permute-start | bytes 1179656 | tf_op jit(solution)/shard_map/ppermute | solution.py:37
  10.9 28.3 %collective-permute-start.6 = (bf16[4,3,128,128]{3,2,1,0:T(8,128)(2,1)}, bf16[4,3,128,128]{3,2,1,0:T(8,128)(2,1)S(1)}, u32[]{:S(2)}, u32[]{:S(2)}) collective-permute-start(bf16[4,3,128,128]{3,2,1,0:T(8,128)(2,1)} %get-tuple-element.49), channel_id=1, source_target_pairs={{0,3},{1,2},{2,1},{3,0},{4,7},{5,6},{6,5},{7,4},{8,11},{9,10},{10,... | collective-permute-start | bytes 1179656 | tf_op jit(solution)/shard_map/ppermute | solution.py:37
  10.9 28.9 %collective-permute-start.7 = (bf16[4,3,128,128]{3,2,1,0:T(8,128)(2,1)}, bf16[4,3,128,128]{3,2,1,0:T(8,128)(2,1)S(1)}, u32[]{:S(2)}, u32[]{:S(2)}) collective-permute-start(bf16[4,3,128,128]{3,2,1,0:T(8,128)(2,1)} %get-tuple-element.50), channel_id=1, source_target_pairs={{0,4},{1,5},{2,6},{3,7},{4,0},{5,1},{6,2},{7,3},{8,12},{9,13},{10,... | collective-permute-start | bytes 1179656 | tf_op jit(solution)/shard_map/ppermute | solution.py:37
  12.4 37.9 %copy-start.6 = (bf16[4,3,128,128]{3,2,1,0:T(8,128)(2,1)}, bf16[4,3,128,128]{3,2,1,0:T(8,128)(2,1)S(1)}, u32[]{:S(2)}) copy-start(bf16[4,3,128,128]{3,2,1,0:T(8,128)(2,1)S(1)} %collective-permute-done.4.refs_1_.refs_6_) | copy-start | bytes 1179652
  12.4 35.1 %collective-permute-start.8 = (bf16[4,3,128,128]{3,2,1,0:T(8,128)(2,1)}, bf16[4,3,128,128]{3,2,1,0:T(8,128)(2,1)}, u32[]{:S(2)}, u32[]{:S(2)}) collective-permute-start(bf16[4,3,128,128]{3,2,1,0:T(8,128)(2,1)} %get-tuple-element.51), channel_id=1, source_target_pairs={{0,5},{1,4},{2,7},{3,6},{4,1},{5,0},{6,3},{7,2},{8,13},{9,12},{10,... | collective-permute-start | bytes 1179656 | tf_op jit(solution)/shard_map/ppermute | solution.py:37
  20.8 29.6 %copy-start.7 = (bf16[4,3,128,128]{3,2,1,0:T(8,128)(2,1)}, bf16[4,3,128,128]{3,2,1,0:T(8,128)(2,1)S(1)}, u32[]{:S(2)}) copy-start(bf16[4,3,128,128]{3,2,1,0:T(8,128)(2,1)S(1)} %collective-permute-done.5.refs_2_.refs_7_) | copy-start | bytes 1179652
  20.8 29.6 %collective-permute-start.9 = (bf16[4,3,128,128]{3,2,1,0:T(8,128)(2,1)}, bf16[4,3,128,128]{3,2,1,0:T(8,128)(2,1)}, u32[]{:S(2)}, u32[]{:S(2)}) collective-permute-start(bf16[4,3,128,128]{3,2,1,0:T(8,128)(2,1)} %get-tuple-element.52), channel_id=1, source_target_pairs={{0,6},{1,7},{2,4},{3,5},{4,2},{5,3},{6,0},{7,1},{8,14},{9,15},{10,... | collective-permute-start | bytes 1179656 | tf_op jit(solution)/shard_map/ppermute | solution.py:37
  23.8 11.3 %copy-start.1 = (bf16[4,4,3,128,128]{4,3,2,1,0:T(8,128)(2,1)}, bf16[4,4,3,128,128]{4,3,2,1,0:T(8,128)(2,1)S(1)}, u32[]{:S(2)}) copy-start(bf16[4,4,3,128,128]{4,3,2,1,0:T(8,128)(2,1)S(1)} %collective-permute-done.refs_3_) | copy-start | bytes 4718596
  23.8 26.5 %collective-permute-start.10 = (bf16[4,3,128,128]{3,2,1,0:T(8,128)(2,1)}, bf16[4,3,128,128]{3,2,1,0:T(8,128)(2,1)}, u32[]{:S(2)}, u32[]{:S(2)}) collective-permute-start(bf16[4,3,128,128]{3,2,1,0:T(8,128)(2,1)} %get-tuple-element.53), channel_id=1, source_target_pairs={{0,7},{1,6},{2,5},{3,4},{4,3},{5,2},{6,1},{7,0},{8,15},{9,14},{10,... | collective-permute-start | bytes 1179656 | tf_op jit(solution)/shard_map/ppermute | solution.py:37
  24.5 10.6 %all-to-all-start = ((f32[4,4,1024]{2,1,0:T(4,128)}), f32[4,4,1024]{2,1,0:T(4,128)S(1)}, u32[]{:S(2)}, u32[]{:S(2)}) async-start(f32[4,4,1024]{2,1,0:T(4,128)} %broadcast_in_dim.3), calls=%async_computation | async-start | bytes 131072 | tf_op jit(solution)/shard_map/all_to_all | solution.py:463
  35.1 4.0 %copy-start.3 = (f32[4,4,1024]{2,1,0:T(4,128)}, f32[4,4,1024]{2,1,0:T(4,128)S(1)}, u32[]{:S(2)}) copy-start(f32[4,4,1024]{2,1,0:T(4,128)S(1)} %all-to-all-done.refs_8_.refs_13_.gain_ref) | copy-start | bytes 196612
  39.2 11.2 %copy-start.8 = (bf16[4,3,128,128]{3,2,1,0:T(8,128)(2,1)}, bf16[4,3,128,128]{3,2,1,0:T(8,128)(2,1)S(1)}, u32[]{:S(2)}) copy-start(bf16[4,3,128,128]{3,2,1,0:T(8,128)(2,1)S(1)} %collective-permute-done.6.refs_3_.refs_8_) | copy-start | bytes 1179652
  39.2 21.3 %collective-permute-start.1 = (bf16[2,2,3,128,128]{4,3,2,1,0:T(8,128)(2,1)}, bf16[2,2,3,128,128]{4,3,2,1,0:T(8,128)(2,1)S(1)}, u32[]{:S(2)}, u32[]{:S(2)}) collective-permute-start(bf16[2,2,3,128,128]{4,3,2,1,0:T(8,128)(2,1)} %get-tuple-element.61), channel_id=1, source_target_pairs={{0,2},{1,3},{2,0},{3,1},{4,6},{5,7},{6,4},{7,5},{8,10},{9,11},{10,... | collective-permute-start | bytes 1179656 | tf_op jit(solution)/shard_map/ppermute | solution.py:37
  39.8 10.6 %copy-start.9 = (bf16[4,3,128,128]{3,2,1,0:T(8,128)(2,1)}, bf16[4,3,128,128]{3,2,1,0:T(8,128)(2,1)S(1)}, u32[]{:S(2)}) copy-start(bf16[4,3,128,128]{3,2,1,0:T(8,128)(2,1)S(1)} %collective-permute-done.7.refs_4_.refs_9_) | copy-start | bytes 1179652
  39.8 25.4 %collective-permute-start.2 = (bf16[2,2,3,128,128]{4,3,2,1,0:T(8,128)(2,1)}, bf16[2,2,3,128,128]{4,3,2,1,0:T(8,128)(2,1)S(1)}, u32[]{:S(2)}, u32[]{:S(2)}) collective-permute-start(bf16[2,2,3,128,128]{4,3,2,1,0:T(8,128)(2,1)} %get-tuple-element.67), channel_id=1, source_target_pairs={{0,4},{1,5},{2,6},{3,7},{4,0},{5,1},{6,2},{7,3},{8,12},{9,13},{10,... | collective-permute-start | bytes 1179656 | tf_op jit(solution)/shard_map/ppermute | solution.py:37
  47.5 13.7 %copy-start.10 = (bf16[2,2,3,128,128]{4,3,2,1,0:T(8,128)(2,1)S(1)}, bf16[2,2,3,128,128]{4,3,2,1,0:T(8,128)(2,1)}, u32[]{:S(2)}) copy-start(bf16[2,2,3,128,128]{4,3,2,1,0:T(8,128)(2,1)} %get-tuple-element.75) | copy-start | bytes 1179652
  47.5 17.6 %collective-permute-start.3 = (bf16[2,2,3,128,128]{4,3,2,1,0:T(8,128)(2,1)}, bf16[2,2,3,128,128]{4,3,2,1,0:T(8,128)(2,1)S(1)}, u32[]{:S(2)}, u32[]{:S(2)}) collective-permute-start(bf16[2,2,3,128,128]{4,3,2,1,0:T(8,128)(2,1)} %get-tuple-element.68), channel_id=1, source_target_pairs={{0,6},{1,7},{2,4},{3,5},{4,2},{5,3},{6,0},{7,1},{8,14},{9,15},{10,... | collective-permute-start | bytes 1179656 | tf_op jit(solution)/shard_map/ppermute | solution.py:37
  60.5 3.6 %copy-start.11 = (bf16[2,2,3,128,128]{4,3,2,1,0:T(8,128)(2,1)}, bf16[2,2,3,128,128]{4,3,2,1,0:T(8,128)(2,1)S(1)}, u32[]{:S(2)}) copy-start(bf16[2,2,3,128,128]{4,3,2,1,0:T(8,128)(2,1)S(1)} %collective-permute-done.1.refs_2_) | copy-start | bytes 1179652
  60.5 19.7 %collective-permute-start.11 = (bf16[2,2,3,128,128]{4,3,2,1,0:T(8,128)(2,1)}, bf16[2,2,3,128,128]{4,3,2,1,0:T(8,128)(2,1)S(1)}, u32[]{:S(2)}, u32[]{:S(2)}) collective-permute-start(bf16[2,2,3,128,128]{4,3,2,1,0:T(8,128)(2,1)} %get-tuple-element.73), channel_id=1, source_target_pairs={{0,2},{1,3},{2,0},{3,1},{4,6},{5,7},{6,4},{7,5},{8,10},{9,11},{10,... | collective-permute-start | bytes 1179656 | tf_op jit(solution)/shard_map/ppermute | solution.py:37
  61.0 21.0 %collective-permute-start.12 = (bf16[2,2,3,128,128]{4,3,2,1,0:T(8,128)(2,1)}, bf16[2,2,3,128,128]{4,3,2,1,0:T(8,128)(2,1)S(1)}, u32[]{:S(2)}, u32[]{:S(2)}) collective-permute-start(bf16[2,2,3,128,128]{4,3,2,1,0:T(8,128)(2,1)} %get-tuple-element.74), channel_id=1, source_target_pairs={{0,4},{1,5},{2,6},{3,7},{4,0},{5,1},{6,2},{7,3},{8,12},{9,13},{10,... | collective-permute-start | bytes 1179656 | tf_op jit(solution)/shard_map/ppermute | solution.py:37
  61.2 20.8 %collective-permute-start.13 = (bf16[2,2,3,128,128]{4,3,2,1,0:T(8,128)(2,1)S(1)}, bf16[2,2,3,128,128]{4,3,2,1,0:T(8,128)(2,1)S(1)}, u32[]{:S(2)}, u32[]{:S(2)}) collective-permute-start(bf16[2,2,3,128,128]{4,3,2,1,0:T(8,128)(2,1)S(1)} %copy-done.10), channel_id=1, source_target_pairs={{0,6},{1,7},{2,4},{3,5},{4,2},{5,3},{6,0},{7,1},{8,14},{9,15},{10,... | collective-permute-start | bytes 1179656 | tf_op jit(solution)/shard_map/ppermute | solution.py:37
  65.2 3.8 %copy-start.12 = (bf16[2,2,3,128,128]{4,3,2,1,0:T(8,128)(2,1)}, bf16[2,2,3,128,128]{4,3,2,1,0:T(8,128)(2,1)S(1)}, u32[]{:S(2)}) copy-start(bf16[2,2,3,128,128]{4,3,2,1,0:T(8,128)(2,1)S(1)} %collective-permute-done.2.refs_3_) | copy-start | bytes 1179652
  65.2 3.8 %copy-start.15 = (bf16[2,2,3,128,128]{4,3,2,1,0:T(8,128)(2,1)}, bf16[2,2,3,128,128]{4,3,2,1,0:T(8,128)(2,1)S(1)}, u32[]{:S(2)}) copy-start(bf16[2,2,3,128,128]{4,3,2,1,0:T(8,128)(2,1)S(1)} %collective-permute-done.3.refs_4_) | copy-start | bytes 1179652
  65.2 29.7 %all-to-all-start.1 = ((bf16[8,4,128,128]{3,2,1,0:T(8,128)(2,1)}), bf16[8,4,128,128]{3,2,1,0:T(8,128)(2,1)S(1)}, u32[]{:S(2)}, u32[]{:S(2)}) async-start(bf16[8,4,128,128]{3,2,1,0:T(8,128)(2,1)} %get-tuple-element.71.refs_14_), calls=%async_computation.1 | async-start | bytes 2097152 | tf_op jit(solution)/shard_map/all_to_all | solution.py:433
  94.9 8.9 %copy-start = (bf16[8,4,128,128]{3,2,1,0:T(8,128)(2,1)}, bf16[8,4,128,128]{3,2,1,0:T(8,128)(2,1)S(1)}, u32[]{:S(2)}) copy-start(bf16[8,4,128,128]{3,2,1,0:T(8,128)(2,1)S(1)} %all-to-all-done.1.parts_ref) | copy-start | bytes 3145732
  94.9 19.5 %all-to-all-start.2 = ((f32[32,4,512]{2,1,0:T(4,128)}), f32[32,4,512]{2,1,0:T(4,128)S(1)}, u32[]{:S(2)}, u32[]{:S(2)}) async-start(f32[32,4,512]{2,1,0:T(4,128)} %teacher.3), calls=%async_computation.2 | async-start | bytes 524288 | tf_op jit(solution)/shard_map/all_to_all | solution.py:494
  (4 other events, 4.1 us)

commit v3 on v2

--- a/solution.py
+++ b/solution.py
@@ -15,10 +15,11 @@
 step_size = 0.01
 ema_decay = 0.95
 
-VMEM_BYTES = 60 * 1024 * 1024
+VMEM_BYTES = 62 * 1024 * 1024
 STUDENT_BLOCK = 512
 TEACHER_BLOCK = 512
 TERMS = 4
+PREP_ROWS = 64
 
 f32 = jnp.float32
 bf16 = jnp.bfloat16
@@ -39,59 +40,6 @@
 
 def nn(a, b):
     return lax.dot_general(a, b, (((1,), (0,)), ((), ())), preferred_element_type=f32)
-
-
-def prep_kernel(groups, width, plans, *refs):
-    ins, outs = refs[:3], refs[3:]
-    me = lax.axis_index("seq")
-    inverse = []
-    for x_ref in ins[:2]:
-        wide = x_ref[...].astype(f32)
-        inverse.append(lax.rsqrt(jnp.mean(wide * wide, axis=-1, keepdims=True) + norm_eps))
-
-    at = 0
-    for first, columns, by_step in plans:
-        for slot in range(groups):
-            if by_step:
-                col = pl.multiple_of((me ^ slot) * width + first, HEAD_DIM)
-            else:
-                col = slot * width + first
-            for a in range(3):
-                part = ins[a][:, pl.ds(col, columns)]
-                if a < 2:
-                    part = (part.astype(f32) * inverse[a]).astype(bf16)
-                for h in range(columns // HEAD_DIM):
-                    head = part[:, h * HEAD_DIM : (h + 1) * HEAD_DIM]
-                    if by_step:
-                        outs[at + slot][h, a] = head
-                    else:
-                        outs[at][slot, h, a] = head
-        at += groups if by_step else 1
-
-
-def prep(q, k, v, groups, width, plans):
-    tokens, inner = q.shape
-    rows = min(64, tokens)
-    shapes, specs = [], []
-    for _, columns, by_step in plans:
-        heads = columns // HEAD_DIM
-        if by_step:
-            for _ in range(groups):
-                shapes.append(jax.ShapeDtypeStruct((heads, 3, tokens, HEAD_DIM), bf16))
-                specs.append(pl.BlockSpec((heads, 3, rows, HEAD_DIM), lambda i: (0, 0, i, 0)))
-        else:
-            shapes.append(jax.ShapeDtypeStruct((groups, heads, 3, tokens, HEAD_DIM), bf16))
-            specs.append(pl.BlockSpec((groups, heads, 3, rows, HEAD_DIM), lambda i: (0, 0, 0, i, 0)))
-    return pl.pallas_call(
-        functools.partial(prep_kernel, groups, width, plans),
-        grid=(tokens // rows,),
-        in_specs=[pl.BlockSpec((rows, inner), lambda i: (i, 0))] * 3,
-        out_specs=specs,
-        out_shape=shapes,
-        compiler_params=params(),
-        cost_estimate=cost(20 * tokens * inner, 12 * tokens * inner),
-        name="prep",
-    )(q, k, v)
 
 
 def scales(refs):
@@ -107,15 +55,39 @@
     return (part.astype(f32) * inverse[a]).astype(bf16) if a < 2 else part
 
 
-def sibling_kernel(groups, width, *refs):
-    ins, out_ref = refs[:3], refs[3]
+def prep_kernel(groups, width, *refs):
+    student_ins, teacher_ins, outs, near_ref = refs[:3], refs[3:6], refs[6:-1], refs[-1]
     me = lax.axis_index("seq")
-    inverse = scales(ins[:2])
+    inverse = scales(student_ins[:2])
+    for slot in range(groups):
+        for h in range(width // HEAD_DIM):
+            col = pl.multiple_of((me ^ slot) * width + h * HEAD_DIM, HEAD_DIM)
+            for a in range(3):
+                outs[slot][h, a] = unit_part(student_ins, inverse, a, col)
+    inverse = scales(teacher_ins[:2])
     for pair in range(groups // 2):
         for h in range(width // HEAD_DIM):
             col = pl.multiple_of((me ^ (2 * pair + 1)) * width + h * HEAD_DIM, HEAD_DIM)
             for a in range(3):
-                out_ref[pair, h, a] = unit_part(ins, inverse, a, col)
+                near_ref[pair, h, a] = unit_part(teacher_ins, inverse, a, col)
+
+
+def prep(student_ins, teacher_ins, groups, width):
+    tokens, inner = student_ins[0].shape
+    heads = width // HEAD_DIM
+    rows = min(PREP_ROWS, tokens)
+    return pl.pallas_call(
+        functools.partial(prep_kernel, groups, width),
+        grid=(tokens // rows,),
+        in_specs=[pl.BlockSpec((rows, inner), lambda i: (i, 0))] * 6,
+        out_specs=[pl.BlockSpec((heads, 3, rows, HEAD_DIM), lambda i: (0, 0, i, 0))] * groups
+        + [pl.BlockSpec((groups // 2, heads, 3, rows, HEAD_DIM), lambda i: (0, 0, 0, i, 0))],
+        out_shape=[jax.ShapeDtypeStruct((heads, 3, tokens, HEAD_DIM), bf16)] * groups
+        + [jax.ShapeDtypeStruct((groups // 2, heads, 3, tokens, HEAD_DIM), bf16)],
+        compiler_params=params(),
+        cost_estimate=cost(40 * tokens * inner, 21 * tokens * inner),
+        name="prep",
+    )(*student_ins, *teacher_ins)
 
 
 def pair_kernel(groups, width, counts, *refs):
@@ -137,21 +109,9 @@
 def prep_pairs(q, k, v, groups, width, counts, near):
     tokens, inner = q.shape
     heads = width // HEAD_DIM
-    rows = min(64, tokens)
+    rows = min(PREP_ROWS, tokens)
     in_specs = [pl.BlockSpec((rows, inner), lambda i: (i, 0))] * 3
     near_spec = pl.BlockSpec((groups // 2, heads, 3, rows, HEAD_DIM), lambda i: (0, 0, 0, i, 0))
-    near_shape = jax.ShapeDtypeStruct((groups // 2, heads, 3, tokens, HEAD_DIM), bf16)
-    if near is None:
-        return pl.pallas_call(
-            functools.partial(sibling_kernel, groups, width),
-            grid=(tokens // rows,),
-            in_specs=in_specs,
-            out_specs=near_spec,
-            out_shape=near_shape,
-            compiler_params=params(),
-            cost_estimate=cost(20 * tokens * inner, 9 * tokens * inner),
-            name="prep_near",
-        )(q, k, v)
     shapes, specs = [], []
     for count in counts:
         for _ in range(groups // 2):
@@ -417,6 +377,10 @@
     )(parts)
 
 
+def chunk_heads(heads):
+    return (heads - heads // 2, heads // 2) if heads > 1 else (1,)
+
+
 def by_step(parts):
     size = len(parts)
     received = list(parts)
@@ -450,45 +414,33 @@
     inner = query_teacher.shape[2]
     width = inner // groups
     heads = width // HEAD_DIM
-    split = (heads + 1) // 2 * HEAD_DIM
-
-    sent = prep(query_student[0], key_student[0], value_student[0], groups, width, [(0, width, True)])
+
+    later = [query_teacher[0], key_teacher[0], value_teacher[0]]
+    counts = chunk_heads(heads)
+    *sent, near = prep([query_student[0], key_student[0], value_student[0]], later, groups, width)
     student_parts = by_step(sent)
-    sent, later = lax.optimization_barrier((sent, (query_teacher, key_teacher, value_teacher)))
-    later = [x[0] for x in later]
-    counts = (split // HEAD_DIM, heads - split // HEAD_DIM)
-    near = prep_pairs(*later, groups, width, counts, None)
-    near, own_gains = lax.optimization_barrier((near, jnp.concatenate([student_gain, ema_gain], axis=0)))
+    near, *own_gains = lax.optimization_barrier((near, student_gain, ema_gain))
+    own_gains = jnp.concatenate(own_gains, axis=0)
     own_gains = jnp.broadcast_to(own_gains, (clips, *own_gains.shape))
     gains = lax.all_to_all(own_gains, "fsdp", split_axis=0, concat_axis=0, tiled=True)
     near, gains = lax.optimization_barrier((swap(near, "seq", 1), gains))
     sent = prep_pairs(*later, groups, width, counts, near)
-    first_sent, second_sent = sent[: groups // 2], sent[groups // 2 :]
-    teacher_first = by_pairs(first_sent)
-    ahead, second_sent = lax.optimization_barrier((teacher_first[1], second_sent))
-    teacher_first[1] = ahead
-    teacher_second = by_pairs(second_sent)
+    pairs = groups // 2
+    chunks = [by_pairs(sent[:pairs])]
+    for i in range(1, len(counts)):
+        ahead, going = lax.optimization_barrier((chunks[-1][1], sent[i * pairs : (i + 1) * pairs]))
+        chunks[-1][1] = ahead
+        chunks.append(by_pairs(going))
     out, lse = student(student_parts, gains, groups, tokens, width)
-    teacher_first, going = lax.optimization_barrier((teacher_first, out))
+    chunks[0], going = lax.optimization_barrier((chunks[0], out))
     returned = by_source(going)[0]
-    grads = teacher(
-        timesteps, teacher_first, student_parts, gains, out, lse, None, 0, split // HEAD_DIM, groups, tokens, width, 1
-    )
-    grads = teacher(
-        timesteps,
-        teacher_second,
-        student_parts,
-        gains,
-        out,
-        lse,
-        grads,
-        split // HEAD_DIM,
-        heads - split // HEAD_DIM,
-        groups,
-        tokens,
-        width,
-        clips * groups,
-    )
+    grads, first = None, 0
+    for i, count in enumerate(counts):
+        copies = clips * groups if i == len(counts) - 1 else 1
+        grads = teacher(
+            timesteps, chunks[i], student_parts, gains, out, lse, grads, first, count, groups, tokens, width, copies
+        )
+        first += count
     returned, grads = lax.optimization_barrier((returned, grads))
     student_out = assemble(returned)
     terms = lax.all_to_all(grads, ("fsdp", "seq"), split_axis=0, concat_axis=0, tiled=True)

time: 117 us -> 115 us (0.983)
  waiting for transfers between devices: 29.1 us -> 27.7 us
  Pallas kernels: 48.5 us -> 47.2 us
    pallas_call x2 -> x1, Pallas kernels: 6.73 us -> 5.4 us  [prep(): pl.pallas_call(functools.partial(prep_kernel, groups, width), grid=(token...]
    ppermute x14, waiting for transfers between devices: 16.8 us -> 15.5 us  [swap(): return lax.ppermute(x, axis, [(i, i ^ step) for i in range(size)])]
  transfers between devices with their start and end apart: 17 -> 17, of which waited for: 6 -> 6; matrix products, arithmetic and copies ran while one was open for 1% -> 1% of each run, Pallas kernels for 34% -> 35%
where the time goes in v3:
time: 115 us; the launch traced here: 114 us
  Pallas kernels  47.2 us (41%)
  starting transfers between devices  35.2 us (31%)
  waiting for transfers between devices  27.7 us (24%)
  local copies, waits for them, and re-layouts  2.25 us (2%)
  between operations  1.62 us (1%)
    pallas_call x2, Pallas kernels, teacher(): pl.pallas_call(functools.partial(teacher_kernel, groups, tokens, width, f...  22.5 us
    ppermute x14, starting transfers between devices, swap(): return lax.ppermute(x, axis, [(i, i ^ step) for i in range(size)])  17.9 us
    ppermute x14, waiting for transfers between devices, swap(): return lax.ppermute(x, axis, [(i, i ^ step) for i in range(size)])  15.5 us
    pallas_call x1, Pallas kernels, student(): pl.pallas_call(functools.partial(student_kernel, groups, tokens, width, l...  10.1 us
    all_to_all x1, starting transfers between devices, local(): lax.all_to_all(grads, ('fsdp', 'seq'), split_axis=0, concat_axis=0, tiled...  8.66 us
    all_to_all x1, waiting for transfers between devices, local(): lax.all_to_all(grads, ('fsdp', 'seq'), split_axis=0, concat_axis=0, tiled...  7.15 us
    pallas_call x1, Pallas kernels, prep(): pl.pallas_call(functools.partial(prep_kernel, groups, width), grid=(token...  5.4 us
    all_to_all x1, waiting for transfers between devices, local(): lax.all_to_all(own_gains, 'fsdp', split_axis=0, concat_axis=0, tiled=True)  5.09 us
  transfers between devices with their start and end apart: 17, of which 6 were waited for; matrix products, arithmetic and copies ran while one was open for 1% of the time, Pallas kernels for 35%

profile of v3, /device:TPU:0, one launch (start us, length us, event | category | flops | bytes accessed | tf_op | source)
XLA Modules:
  0.0 114.0 jit_solution(16301030230065152647)
XLA Ops:
  0.7 5.4 %prep.1 = (bf16[4,3,128,128]{3,2,1,0:T(8,128)(2,1)}, bf16[4,3,128,128]{3,2,1,0:T(8,128)(2,1)}, bf16[4,3,128,128]{3,2,1,0:T(8,128)(2,1)}, bf16[4,3,128,128]{3,2,1...) custom-call(bf16[128,4096]{1,0:T(8,128)(2,1)} %bitcast.12, ...), custom_call_target="tpu_custom_call" | custom-call | flops 20971520 | bytes 11010048 | tf_op jit(solution)/shard_map/prep/pallas_call | solution.py:79
  6.1 0.5 collective-permute-start
  6.6 0.1 collective-permute-start.4
  6.7 2.9 %collective-permute-start.5 = (bf16[4,3,128,128]{3,2,1,0:T(8,128)(2,1)}, bf16[4,3,128,128]{3,2,1,0:T(8,128)(2,1)S(1)}, u32[]{:S(2)}, u32[]{:S(2)}) collective-permute-start(bf16[4,3,128,128]{3,2,1,0:T(8,128)(2,1)} %get-tuple-element.61), channel_id=1, source_target_pairs={{0,2},{1,3},{2,0},{3,1},{4,6},{5,7},{6,4},{7,5},{8,10},{9,11},{10,... | collective-permute-start | bytes 1179656 | tf_op jit(solution)/shard_map/ppermute | solution.py:38
  9.6 1.5 %collective-permute-start.7 = (bf16[4,3,128,128]{3,2,1,0:T(8,128)(2,1)}, bf16[4,3,128,128]{3,2,1,0:T(8,128)(2,1)}, u32[]{:S(2)}, u32[]{:S(2)}) collective-permute-start(bf16[4,3,128,128]{3,2,1,0:T(8,128)(2,1)} %get-tuple-element.63), channel_id=1, source_target_pairs={{0,4},{1,5},{2,6},{3,7},{4,0},{5,1},{6,2},{7,3},{8,12},{9,13},{10,... | collective-permute-start | bytes 1179656 | tf_op jit(solution)/shard_map/ppermute | solution.py:38
  11.1 1.9 %collective-permute-start.8 = (bf16[4,3,128,128]{3,2,1,0:T(8,128)(2,1)}, bf16[4,3,128,128]{3,2,1,0:T(8,128)(2,1)}, u32[]{:S(2)}, u32[]{:S(2)}) collective-permute-start(bf16[4,3,128,128]{3,2,1,0:T(8,128)(2,1)} %get-tuple-element.64), channel_id=1, source_target_pairs={{0,5},{1,4},{2,7},{3,6},{4,1},{5,0},{6,3},{7,2},{8,13},{9,12},{10,... | collective-permute-start | bytes 1179656 | tf_op jit(solution)/shard_map/ppermute | solution.py:38
  13.0 6.7 %collective-permute-done.5.refs_2_.refs_7_ = bf16[4,3,128,128]{3,2,1,0:T(8,128)(2,1)S(1)} collective-permute-done((bf16[4,3,128,128]{3,2,1,0:T(8,128)(2,1)}, bf16[4,3,128,128]{3,2,1,0:T(8,128)(2,1)S(1)}, u32[]{:S(2)}, u32[]{:S(2)}) %collective-permute-start.5) | collective-permute-done | bytes 393248 | tf_op jit(solution)/shard_map/ppermute | solution.py:38
  19.7 3.0 %collective-permute-start.9 = (bf16[4,3,128,128]{3,2,1,0:T(8,128)(2,1)}, bf16[4,3,128,128]{3,2,1,0:T(8,128)(2,1)}, u32[]{:S(2)}, u32[]{:S(2)}) collective-permute-start(bf16[4,3,128,128]{3,2,1,0:T(8,128)(2,1)} %get-tuple-element.65), channel_id=1, source_target_pairs={{0,6},{1,7},{2,4},{3,5},{4,2},{5,3},{6,0},{7,1},{8,14},{9,15},{10,... | collective-permute-start | bytes 1179656 | tf_op jit(solution)/shard_map/ppermute | solution.py:38
  22.7 0.1 collective-permute-start.10
  22.8 0.8 broadcast_in_dim.3
  23.6 4.9 %all-to-all-start = ((f32[4,4,1024]{2,1,0:T(4,128)}), f32[4,4,1024]{2,1,0:T(4,128)S(1)}, u32[]{:S(2)}, u32[]{:S(2)}) async-start(f32[4,4,1024]{2,1,0:T(4,128)} %broadcast_in_dim.3), calls=%async_computation | async-start | bytes 131072 | tf_op jit(solution)/shard_map/all_to_all | solution.py:425
  29.1 5.1 %all-to-all-done.refs_8_.refs_13_.gain_ref = f32[4,4,1024]{2,1,0:T(4,128)S(1)} async-done(((f32[4,4,1024]{2,1,0:T(4,128)}), f32[4,4,1024]{2,1,0:T(4,128)S(1)}, u32[]{:S(2)}, u32[]{:S(2)}) %all-to-all-start) | async-done | bytes 65568 | tf_op jit(solution)/shard_map/all_to_all | solution.py:425
  34.2 4.0 %prep_pairs.1 = (bf16[2,2,3,128,128]{4,3,2,1,0:T(8,128)(2,1)}, bf16[2,2,3,128,128]{4,3,2,1,0:T(8,128)(2,1)}, bf16[2,2,3,128,128]{4,3,2,1,0:T(8,128)(2,1)}, bf16[...) custom-call(bf16[128,4096]{1,0:T(8,128)(2,1)} %bitcast.7, ...), custom_call_target="tpu_custom_call" | custom-call | flops 10485760 | bytes 7864320 | tf_op jit(solution)/shard_map/prep_pairs/pallas_call | solution.py:120
  38.3 0.6 collective-permute-start.1
  38.9 0.8 collective-permute-start.2
  39.8 6.4 %collective-permute-done.8.refs_5_.refs_10_ = bf16[4,3,128,128]{3,2,1,0:T(8,128)(2,1)} collective-permute-done((bf16[4,3,128,128]{3,2,1,0:T(8,128)(2,1)}, bf16[4,3,128,128]{3,2,1,0:T(8,128)(2,1)}, u32[]{:S(2)}, u32[]{:S(2)}) %collective-permute-start.8) | collective-permute-done | bytes 393248 | tf_op jit(solution)/shard_map/ppermute | solution.py:38
  46.2 2.8 %collective-permute-start.3 = (bf16[2,2,3,128,128]{4,3,2,1,0:T(8,128)(2,1)}, bf16[2,2,3,128,128]{4,3,2,1,0:T(8,128)(2,1)}, u32[]{:S(2)}, u32[]{:S(2)}) collective-permute-start(bf16[2,2,3,128,128]{4,3,2,1,0:T(8,128)(2,1)} %get-tuple-element.58), channel_id=1, source_target_pairs={{0,6},{1,7},{2,4},{3,5},{4,2},{5,3},{6,0},{7,1},{8,14},{9,15},{10,... | collective-permute-start | bytes 1179656 | tf_op jit(solution)/shard_map/ppermute | solution.py:38
  49.0 10.1 %student.1 = (bf16[8,4,128,128]{3,2,1,0:T(8,128)(2,1)}, f32[4,1024,128]{2,1,0:T(8,128)}) custom-call(bf16[4,3,128,128]{3,2,1,0:T(8,128)(2,1)} %get-tuple-element.59.refs_0_.refs_5_, bf16[4,3,128,128]{3,2,1,0:T(8,128)(2,1)} %copy-done.6, bf16[4,3,128,128]{3,2,1,0:T(8,128)(2,1)} %copy-done.7, bf16[4,3,128,128]{3,2,1,0:T(8,128)(2,1)} %collective-permute-done.6.refs_3_.refs_8_, ...), custom_call_target="tpu_custom_call" | custom-call | flops 4294967296 | bytes 4194304 | tf_op jit(solution)/shard_map/student/pallas_call | solution.py:201
  59.2 0.6 collective-permute-start.11
  59.7 0.2 collective-permute-start.12
  59.9 2.8 %collective-permute-start.13 = (bf16[2,2,3,128,128]{4,3,2,1,0:T(8,128)(2,1)S(1)}, bf16[2,2,3,128,128]{4,3,2,1,0:T(8,128)(2,1)}, u32[]{:S(2)}, u32[]{:S(2)}) collective-permute-start(bf16[2,2,3,128,128]{4,3,2,1,0:T(8,128)(2,1)S(1)} %copy-done.8), channel_id=1, source_target_pairs={{0,6},{1,7},{2,4},{3,5},{4,2},{5,3},{6,0},{7,1},{8,14},{9,15},{10,... | collective-permute-start | bytes 1179656 | tf_op jit(solution)/shard_map/ppermute | solution.py:38
  62.7 1.1 collective-permute-done.2.refs_3_
  63.9 0.7 copy-done.10
  64.6 3.7 %all-to-all-start.1 = ((bf16[8,4,128,128]{3,2,1,0:T(8,128)(2,1)}), bf16[8,4,128,128]{3,2,1,0:T(8,128)(2,1)S(1)}, u32[]{:S(2)}, u32[]{:S(2)}) async-start(bf16[8,4,128,128]{3,2,1,0:T(8,128)(2,1)} %get-tuple-element.69.refs_14_), calls=%async_computation.1 | async-start | bytes 2097152 | tf_op jit(solution)/shard_map/all_to_all | solution.py:397
  68.3 11.2 %teacher.2.refs_16_ = f32[1,4,512]{2,1,0:T(4,128)} custom-call(s32[1]{0:T(128)S(6)} %copy.14.refs_0_, bf16[2,2,3,128,128]{4,3,2,1,0:T(8,128)(2,1)} %get-tuple-element.75.refs_1_, bf16[2,2,3,128,128]{4,3,2,1,0:T(8,128)(2,1)} %copy-done.9, bf16[2,2,3,128,128]{4,3,2,1,0:T(8,128)(2,1)} %copy-done.10, ...), custom_call_target="tpu_custom_call" | custom-call | flops 6442450944 | bytes 4194304 | tf_op jit(solution)/shard_map/teacher/pallas_call | solution.py:293
  79.5 1.2 %collective-permute-done.12.refs_3_ = bf16[2,2,3,128,128]{4,3,2,1,0:T(8,128)(2,1)} collective-permute-done((bf16[2,2,3,128,128]{4,3,2,1,0:T(8,128)(2,1)}, bf16[2,2,3,128,128]{4,3,2,1,0:T(8,128)(2,1)}, u32[]{:S(2)}, u32[]{:S(2)}) %collective-permute-start.12) | collective-permute-done | bytes 393248 | tf_op jit(solution)/shard_map/ppermute | solution.py:38
  80.8 11.3 %teacher.3 = f32[32,4,512]{2,1,0:T(4,128)} custom-call(s32[1]{0:T(128)S(6)} %copy.14.refs_0_, bf16[2,2,3,128,128]{4,3,2,1,0:T(8,128)(2,1)} %get-tuple-element.70.refs_1_, bf16[2,2,3,128,128]{4,3,2,1,0:T(8,128)(2,1)} %copy-done.11, bf16[2,2,3,128,128]{4,3,2,1,0:T(8,128)(2,1)} %collective-permute-done.12.refs_3_, ...), custom_call_target="tpu_custom_call" | custom-call | flops 6442450944 | bytes 4194304 | tf_op jit(solution)/shard_map/teacher/pallas_call | solution.py:293
  92.2 8.7 %all-to-all-start.2 = ((f32[32,4,512]{2,1,0:T(4,128)}), f32[32,4,512]{2,1,0:T(4,128)S(1)}, u32[]{:S(2)}, u32[]{:S(2)}) async-start(f32[32,4,512]{2,1,0:T(4,128)} %teacher.3), calls=%async_computation.2 | async-start | bytes 524288 | tf_op jit(solution)/shard_map/all_to_all | solution.py:446
  100.8 3.4 %assemble.1 = bf16[1,128,4096]{2,1,0:T(8,128)(2,1)} custom-call(bf16[8,4,128,128]{3,2,1,0:T(8,128)(2,1)} %copy-done), custom_call_target="tpu_custom_call" | custom-call | tf_op jit(solution)/shard_map/assemble/pallas_call | solution.py:369
  104.3 7.2 %all-to-all-done.2.terms_ref = f32[32,4,512]{2,1,0:T(4,128)S(1)} async-done(((f32[32,4,512]{2,1,0:T(4,128)}), f32[32,4,512]{2,1,0:T(4,128)S(1)}, u32[]{:S(2)}, u32[]{:S(2)}) %all-to-all-start.2) | async-done | bytes 262176 | tf_op jit(solution)/shard_map/all_to_all | solution.py:446
  111.4 0.7 copy-done.2
  112.1 1.8 %finish.1 = (f32[1]{0:T(128)}, f32[2,1024]{1,0:T(2,128)}, f32[2,1024]{1,0:T(2,128)}, f32[2,4096]{1,0:T(2,128)}) custom-call(f32[32,4,512]{2,1,0:T(4,128)} %copy-done.2, f32[4,4,1024]{2,1,0:T(4,128)} %copy-done.3), custom_call_target="tpu_custom_call" | custom-call | tf_op jit(solution)/shard_map/finish/pallas_call | solution.py:345
  (35 shorter events, 0.1 us)
Async XLA Ops:
  0.6 22.2 %copy-start.4 = (f32[2,1024]{1,0:T(2,128)S(1)}, f32[2,1024]{1,0:T(2,128)}, u32[]{:S(2)}) copy-start(f32[2,1024]{1,0:T(2,128)} %param.17) | copy-start | bytes 24580
  0.6 22.2 %copy-start.5 = (f32[2,1024]{1,0:T(2,128)S(1)}, f32[2,1024]{1,0:T(2,128)}, u32[]{:S(2)}) copy-start(f32[2,1024]{1,0:T(2,128)} %param.16) | copy-start | bytes 24580
  6.1 16.7 %collective-permute-start = (bf16[4,4,3,128,128]{4,3,2,1,0:T(8,128)(2,1)}, bf16[4,4,3,128,128]{4,3,2,1,0:T(8,128)(2,1)S(1)}, u32[]{:S(2)}, u32[]{:S(2)}) collective-permute-start(bf16[4,4,3,128,128]{4,3,2,1,0:T(8,128)(2,1)} %get-tuple-element.46), channel_id=1, source_target_pairs={{0,1},{1,0},{2,3},{3,2},{4,5},{5,4},{6,7},{7,6},{8,9},{9,8},{10,11... | collective-permute-start | bytes 4718600 | tf_op jit(solution)/shard_map/ppermute | solution.py:38
  6.6 4.5 %collective-permute-start.4 = (bf16[4,3,128,128]{3,2,1,0:T(8,128)(2,1)}, bf16[4,3,128,128]{3,2,1,0:T(8,128)(2,1)S(1)}, u32[]{:S(2)}, u32[]{:S(2)}) collective-permute-start(bf16[4,3,128,128]{3,2,1,0:T(8,128)(2,1)} %get-tuple-element.60), channel_id=1, source_target_pairs={{0,1},{1,0},{2,3},{3,2},{4,5},{5,4},{6,7},{7,6},{8,9},{9,8},{10,11... | collective-permute-start | bytes 1179656 | tf_op jit(solution)/shard_map/ppermute | solution.py:38
  6.7 13.0 %collective-permute-start.5 = (bf16[4,3,128,128]{3,2,1,0:T(8,128)(2,1)}, bf16[4,3,128,128]{3,2,1,0:T(8,128)(2,1)S(1)}, u32[]{:S(2)}, u32[]{:S(2)}) collective-permute-start(bf16[4,3,128,128]{3,2,1,0:T(8,128)(2,1)} %get-tuple-element.61), channel_id=1, source_target_pairs={{0,2},{1,3},{2,0},{3,1},{4,6},{5,7},{6,4},{7,5},{8,10},{9,11},{10,... | collective-permute-start | bytes 1179656 | tf_op jit(solution)/shard_map/ppermute | solution.py:38
  9.6 28.7 %collective-permute-start.6 = (bf16[4,3,128,128]{3,2,1,0:T(8,128)(2,1)}, bf16[4,3,128,128]{3,2,1,0:T(8,128)(2,1)}, u32[]{:S(2)}, u32[]{:S(2)}) collective-permute-start(bf16[4,3,128,128]{3,2,1,0:T(8,128)(2,1)} %get-tuple-element.62), channel_id=1, source_target_pairs={{0,3},{1,2},{2,1},{3,0},{4,7},{5,6},{6,5},{7,4},{8,11},{9,10},{10,... | collective-permute-start | bytes 1179656 | tf_op jit(solution)/shard_map/ppermute | solution.py:38
  9.6 29.4 %collective-permute-start.7 = (bf16[4,3,128,128]{3,2,1,0:T(8,128)(2,1)}, bf16[4,3,128,128]{3,2,1,0:T(8,128)(2,1)}, u32[]{:S(2)}, u32[]{:S(2)}) collective-permute-start(bf16[4,3,128,128]{3,2,1,0:T(8,128)(2,1)} %get-tuple-element.63), channel_id=1, source_target_pairs={{0,4},{1,5},{2,6},{3,7},{4,0},{5,1},{6,2},{7,3},{8,12},{9,13},{10,... | collective-permute-start | bytes 1179656 | tf_op jit(solution)/shard_map/ppermute | solution.py:38
  11.1 37.9 %copy-start.6 = (bf16[4,3,128,128]{3,2,1,0:T(8,128)(2,1)}, bf16[4,3,128,128]{3,2,1,0:T(8,128)(2,1)S(1)}, u32[]{:S(2)}) copy-start(bf16[4,3,128,128]{3,2,1,0:T(8,128)(2,1)S(1)} %collective-permute-done.4.refs_1_.refs_6_) | copy-start | bytes 1179652
  11.1 35.1 %collective-permute-start.8 = (bf16[4,3,128,128]{3,2,1,0:T(8,128)(2,1)}, bf16[4,3,128,128]{3,2,1,0:T(8,128)(2,1)}, u32[]{:S(2)}, u32[]{:S(2)}) collective-permute-start(bf16[4,3,128,128]{3,2,1,0:T(8,128)(2,1)} %get-tuple-element.64), channel_id=1, source_target_pairs={{0,5},{1,4},{2,7},{3,6},{4,1},{5,0},{6,3},{7,2},{8,13},{9,12},{10,... | collective-permute-start | bytes 1179656 | tf_op jit(solution)/shard_map/ppermute | solution.py:38
  19.7 3.0 %copy-start.7 = (bf16[4,3,128,128]{3,2,1,0:T(8,128)(2,1)}, bf16[4,3,128,128]{3,2,1,0:T(8,128)(2,1)S(1)}, u32[]{:S(2)}) copy-start(bf16[4,3,128,128]{3,2,1,0:T(8,128)(2,1)S(1)} %collective-permute-done.5.refs_2_.refs_7_) | copy-start | bytes 1179652
  19.7 29.3 %collective-permute-start.9 = (bf16[4,3,128,128]{3,2,1,0:T(8,128)(2,1)}, bf16[4,3,128,128]{3,2,1,0:T(8,128)(2,1)}, u32[]{:S(2)}, u32[]{:S(2)}) collective-permute-start(bf16[4,3,128,128]{3,2,1,0:T(8,128)(2,1)} %get-tuple-element.65), channel_id=1, source_target_pairs={{0,6},{1,7},{2,4},{3,5},{4,2},{5,3},{6,0},{7,1},{8,14},{9,15},{10,... | collective-permute-start | bytes 1179656 | tf_op jit(solution)/shard_map/ppermute | solution.py:38
  22.7 11.5 %copy-start.1 = (bf16[4,4,3,128,128]{4,3,2,1,0:T(8,128)(2,1)}, bf16[4,4,3,128,128]{4,3,2,1,0:T(8,128)(2,1)S(1)}, u32[]{:S(2)}) copy-start(bf16[4,4,3,128,128]{4,3,2,1,0:T(8,128)(2,1)S(1)} %collective-permute-done.refs_3_) | copy-start | bytes 4718596
  22.7 26.3 %collective-permute-start.10 = (bf16[4,3,128,128]{3,2,1,0:T(8,128)(2,1)}, bf16[4,3,128,128]{3,2,1,0:T(8,128)(2,1)}, u32[]{:S(2)}, u32[]{:S(2)}) collective-permute-start(bf16[4,3,128,128]{3,2,1,0:T(8,128)(2,1)} %get-tuple-element.66), channel_id=1, source_target_pairs={{0,7},{1,6},{2,5},{3,4},{4,3},{5,2},{6,1},{7,0},{8,15},{9,14},{10,... | collective-permute-start | bytes 1179656 | tf_op jit(solution)/shard_map/ppermute | solution.py:38
  23.6 10.6 %all-to-all-start = ((f32[4,4,1024]{2,1,0:T(4,128)}), f32[4,4,1024]{2,1,0:T(4,128)S(1)}, u32[]{:S(2)}, u32[]{:S(2)}) async-start(f32[4,4,1024]{2,1,0:T(4,128)} %broadcast_in_dim.3), calls=%async_computation | async-start | bytes 131072 | tf_op jit(solution)/shard_map/all_to_all | solution.py:425
  34.2 4.0 %copy-start.3 = (f32[4,4,1024]{2,1,0:T(4,128)}, f32[4,4,1024]{2,1,0:T(4,128)S(1)}, u32[]{:S(2)}) copy-start(f32[4,4,1024]{2,1,0:T(4,128)S(1)} %all-to-all-done.refs_8_.refs_13_.gain_ref) | copy-start | bytes 196612
  38.3 20.9 %collective-permute-start.1 = (bf16[2,2,3,128,128]{4,3,2,1,0:T(8,128)(2,1)}, bf16[2,2,3,128,128]{4,3,2,1,0:T(8,128)(2,1)S(1)}, u32[]{:S(2)}, u32[]{:S(2)}) collective-permute-start(bf16[2,2,3,128,128]{4,3,2,1,0:T(8,128)(2,1)} %get-tuple-element.51), channel_id=1, source_target_pairs={{0,2},{1,3},{2,0},{3,1},{4,6},{5,7},{6,4},{7,5},{8,10},{9,11},{10,... | collective-permute-start | bytes 1179656 | tf_op jit(solution)/shard_map/ppermute | solution.py:38
  38.9 24.9 %collective-permute-start.2 = (bf16[2,2,3,128,128]{4,3,2,1,0:T(8,128)(2,1)}, bf16[2,2,3,128,128]{4,3,2,1,0:T(8,128)(2,1)S(1)}, u32[]{:S(2)}, u32[]{:S(2)}) collective-permute-start(bf16[2,2,3,128,128]{4,3,2,1,0:T(8,128)(2,1)} %get-tuple-element.57), channel_id=1, source_target_pairs={{0,4},{1,5},{2,6},{3,7},{4,0},{5,1},{6,2},{7,3},{8,12},{9,13},{10,... | collective-permute-start | bytes 1179656 | tf_op jit(solution)/shard_map/ppermute | solution.py:38
  46.2 17.6 %collective-permute-start.3 = (bf16[2,2,3,128,128]{4,3,2,1,0:T(8,128)(2,1)}, bf16[2,2,3,128,128]{4,3,2,1,0:T(8,128)(2,1)}, u32[]{:S(2)}, u32[]{:S(2)}) collective-permute-start(bf16[2,2,3,128,128]{4,3,2,1,0:T(8,128)(2,1)} %get-tuple-element.58), channel_id=1, source_target_pairs={{0,6},{1,7},{2,4},{3,5},{4,2},{5,3},{6,0},{7,1},{8,14},{9,15},{10,... | collective-permute-start | bytes 1179656 | tf_op jit(solution)/shard_map/ppermute | solution.py:38
  49.0 10.9 %copy-start.8 = (bf16[2,2,3,128,128]{4,3,2,1,0:T(8,128)(2,1)S(1)}, bf16[2,2,3,128,128]{4,3,2,1,0:T(8,128)(2,1)}, u32[]{:S(2)}) copy-start(bf16[2,2,3,128,128]{4,3,2,1,0:T(8,128)(2,1)} %get-tuple-element.73) | copy-start | bytes 1179652
  59.2 4.7 %copy-start.9 = (bf16[2,2,3,128,128]{4,3,2,1,0:T(8,128)(2,1)}, bf16[2,2,3,128,128]{4,3,2,1,0:T(8,128)(2,1)S(1)}, u32[]{:S(2)}) copy-start(bf16[2,2,3,128,128]{4,3,2,1,0:T(8,128)(2,1)S(1)} %collective-permute-done.1.refs_2_) | copy-start | bytes 1179652
  59.2 20.4 %collective-permute-start.11 = (bf16[2,2,3,128,128]{4,3,2,1,0:T(8,128)(2,1)}, bf16[2,2,3,128,128]{4,3,2,1,0:T(8,128)(2,1)S(1)}, u32[]{:S(2)}, u32[]{:S(2)}) collective-permute-start(bf16[2,2,3,128,128]{4,3,2,1,0:T(8,128)(2,1)} %get-tuple-element.71), channel_id=1, source_target_pairs={{0,2},{1,3},{2,0},{3,1},{4,6},{5,7},{6,4},{7,5},{8,10},{9,11},{10,... | collective-permute-start | bytes 1179656 | tf_op jit(solution)/shard_map/ppermute | solution.py:38
  59.7 21.1 %collective-permute-start.12 = (bf16[2,2,3,128,128]{4,3,2,1,0:T(8,128)(2,1)}, bf16[2,2,3,128,128]{4,3,2,1,0:T(8,128)(2,1)}, u32[]{:S(2)}, u32[]{:S(2)}) collective-permute-start(bf16[2,2,3,128,128]{4,3,2,1,0:T(8,128)(2,1)} %get-tuple-element.72), channel_id=1, source_target_pairs={{0,4},{1,5},{2,6},{3,7},{4,0},{5,1},{6,2},{7,3},{8,12},{9,13},{10,... | collective-permute-start | bytes 1179656 | tf_op jit(solution)/shard_map/ppermute | solution.py:38
  59.9 20.9 %collective-permute-start.13 = (bf16[2,2,3,128,128]{4,3,2,1,0:T(8,128)(2,1)S(1)}, bf16[2,2,3,128,128]{4,3,2,1,0:T(8,128)(2,1)}, u32[]{:S(2)}, u32[]{:S(2)}) collective-permute-start(bf16[2,2,3,128,128]{4,3,2,1,0:T(8,128)(2,1)S(1)} %copy-done.8), channel_id=1, source_target_pairs={{0,6},{1,7},{2,4},{3,5},{4,2},{5,3},{6,0},{7,1},{8,14},{9,15},{10,... | collective-permute-start | bytes 1179656 | tf_op jit(solution)/shard_map/ppermute | solution.py:38
  63.8 0.8 copy-start.10
  64.6 27.5 %all-to-all-start.1 = ((bf16[8,4,128,128]{3,2,1,0:T(8,128)(2,1)}), bf16[8,4,128,128]{3,2,1,0:T(8,128)(2,1)S(1)}, u32[]{:S(2)}, u32[]{:S(2)}) async-start(bf16[8,4,128,128]{3,2,1,0:T(8,128)(2,1)} %get-tuple-element.69.refs_14_), calls=%async_computation.1 | async-start | bytes 2097152 | tf_op jit(solution)/shard_map/all_to_all | solution.py:397
  79.5 1.3 %copy-start.11 = (bf16[2,2,3,128,128]{4,3,2,1,0:T(8,128)(2,1)}, bf16[2,2,3,128,128]{4,3,2,1,0:T(8,128)(2,1)S(1)}, u32[]{:S(2)}) copy-start(bf16[2,2,3,128,128]{4,3,2,1,0:T(8,128)(2,1)S(1)} %collective-permute-done.11.refs_2_) | copy-start | bytes 1179652
  92.1 8.7 %copy-start = (bf16[8,4,128,128]{3,2,1,0:T(8,128)(2,1)}, bf16[8,4,128,128]{3,2,1,0:T(8,128)(2,1)S(1)}, u32[]{:S(2)}) copy-start(bf16[8,4,128,128]{3,2,1,0:T(8,128)(2,1)S(1)} %all-to-all-done.1.parts_ref) | copy-start | bytes 3145732
  92.2 19.3 %all-to-all-start.2 = ((f32[32,4,512]{2,1,0:T(4,128)}), f32[32,4,512]{2,1,0:T(4,128)S(1)}, u32[]{:S(2)}, u32[]{:S(2)}) async-start(f32[32,4,512]{2,1,0:T(4,128)} %teacher.3), calls=%async_computation.2 | async-start | bytes 524288 | tf_op jit(solution)/shard_map/all_to_all | solution.py:446
  111.4 0.7 copy-start.2
